TPU v7x, 256 devices: a whole 4x4x8 slice. The times are simulated.
256 devices in a mesh: grp: 4 (over x), blk: 64 (over z, y, core).
Axes of the slice: x: 4, y: 4, z: 8, core: 2. Of those that a mesh axis runs over, the one named last changes fastest.
Arguments:
- embeddings: bfloat16 [32768, 1024], P(('grp', 'blk')), may hold values from -6 to 6
- cluster_ids: int32 [32768], P(('grp', 'blk')), may hold values from 0 to 15, as said below
- row_order: int32 [32768], P(('grp', 'blk')), may hold values from 0 to 32767, each once
Outputs:
- nearest_earlier: float32 [32768], P(('grp', 'blk'))
Inputs may be any that keep to these rules, and one draw needn't show every extreme that they name: `cluster_ids`: in each aligned block of 128 rows (the rows of one device), at most 64 rows have ids with one value of id % 4, and at most 16 rows have one id. For every blk index some value of id % 4 is taken by exactly 64 rows of every block placed on a device with that blk index, each of its 4 ids by exactly 16 of them.
All inputs are finite; a program needn't handle non-finite values.
Results may differ from a plain program's by a relative error of at most 0.0014.
Values may be sent and summed in bfloat16 or wider, within the bound.
A program may use at most 128 MiB of HBM per device.

v0:
```python
import jax
import jax.numpy as jnp
from jax import lax
from jax.sharding import PartitionSpec as P


def unit_rows(embeddings):
    values = embeddings.astype(jnp.float32)
    return (values * lax.rsqrt(jnp.sum(values * values, axis=1, keepdims=True) + 1e-06)).astype(
        jnp.bfloat16
    )


def pair_scores(left, right):
    return lax.dot_general(
        left, right, (((1,), (1,)), ((), ())), preferred_element_type=jnp.float32
    )


def earlier_max(scores, left_cluster, left_order, right_cluster, right_order):
    mask = (left_cluster[:, None] == right_cluster[None, :]) & (left_cluster[:, None] >= 0)
    mask = mask & (right_order[None, :] < left_order[:, None])
    return jnp.max(jnp.where(mask, scores, jnp.float32(-1.0)), axis=1)


def shards(embeddings, cluster_ids, row_order):
    groups = lax.axis_size("grp")
    count = embeddings.shape[0]
    width = embeddings.shape[1]
    capacity = 2 * count // groups
    slots = groups * capacity
    unit = unit_rows(embeddings)
    target = cluster_ids % groups
    onehot = (target[:, None] == jnp.arange(groups)[None, :]).astype(jnp.int32)
    placed = jnp.sum(onehot * (jnp.cumsum(onehot, axis=0) - 1), axis=1)
    slot = target * capacity + placed
    send_unit = (
        jnp.zeros((slots, width), jnp.bfloat16).at[slot].set(unit).reshape(groups, capacity, width)
    )
    send_cluster = (
        jnp.full((slots,), -1, jnp.int32).at[slot].set(cluster_ids).reshape(groups, capacity)
    )
    send_order = jnp.zeros((slots,), jnp.int32).at[slot].set(row_order).reshape(groups, capacity)
    got_unit, got_cluster, got_order = (
        lax.all_to_all(send_unit, "grp", split_axis=0, concat_axis=0, tiled=True),
        lax.all_to_all(send_cluster, "grp", split_axis=0, concat_axis=0, tiled=True),
        lax.all_to_all(send_order, "grp", split_axis=0, concat_axis=0, tiled=True),
    )
    local_unit = got_unit.reshape(slots, width)
    local_cluster = got_cluster.reshape(slots)
    local_order = got_order.reshape(slots)
    initial = jnp.full((slots,), -1.0, jnp.float32)
    piece_unit = lax.all_gather(local_unit, "blk", axis=0, tiled=True)
    piece_cluster = lax.all_gather(local_cluster, "blk", axis=0, tiled=True)
    piece_order = lax.all_gather(local_order, "blk", axis=0, tiled=True)
    scores = pair_scores(local_unit, piece_unit)
    best = jnp.maximum(
        initial, earlier_max(scores, local_cluster, local_order, piece_cluster, piece_order)
    )
    back = lax.all_to_all(
        best.reshape(groups, capacity), "grp", split_axis=0, concat_axis=0, tiled=True
    )
    return back.reshape(slots)[slot]


def solution(mesh):
    in_specs = (P(("grp", "blk"), None), P(("grp", "blk")), P(("grp", "blk")))
    out_specs = P(("grp", "blk"))
    return jax.shard_map(shards, mesh=mesh, in_specs=in_specs, out_specs=out_specs, check_vma=False)
```

profile of v0, /device:TPU:1, one launch (start us, length us, event | category | flops | bytes accessed | tf_op | source)
XLA Modules:
  0.0 205.3 jit_solution(13049572975555639686)
XLA Ops:
  6.5 0.0 all-gather.4.cloned.1.call-start
  6.5 0.7 and_select_fusion
  7.2 0.1 fusion.7
  7.3 0.2 reduce_window_sum.11
  7.5 0.2 select_reduce_fusion
  7.6 0.7 compare_select_fusion
  8.3 1.1 fusion.1
  9.4 1.8 scatter_custom_fusion.2
  11.2 12.7 %all_to_all.29 = bf16[4,64,1024]{2,1,0:T(8,128)(2,1)} all-to-all(bf16[4,64,1024]{2,1,0:T(8,128)(2,1)S(1)} %bitcast.10), channel_id=1, replica_groups=mesh['grp'=4,'blk'=64] {'grp'}, dimensions={0} | all-to-all | bytes 1048576 | tf_op jit(solution)/shard_map/all_to_all | solution.py:45
  23.9 0.0 all-gather.4.cloned.1.call-update
  23.9 1.1 scatter_custom_fusion.1
  25.0 0.7 all_to_all.21
  25.7 3.2 %all-to-all-start.1 = ((s32[4,1,64]{2,1,0:T(1,128)}), s32[4,1,64]{2,1,0:T(1,128)S(1)}, u32[]{:S(2)}, u32[]{:S(2)}) async-start(s32[4,1,64]{2,1,0:T(1,128)} %all_to_all.21), calls=%async_computation.1 | async-start | bytes 4096 | tf_op jit(solution)/shard_map/all_to_all | solution.py:47
  28.9 1.1 scatter_custom_fusion
  30.1 0.7 all_to_all.19
  30.7 2.3 %all-to-all-done.1 = s32[4,1,64]{2,1,0:T(1,128)S(1)} async-done(((s32[4,1,64]{2,1,0:T(1,128)}), s32[4,1,64]{2,1,0:T(1,128)S(1)}, u32[]{:S(2)}, u32[]{:S(2)}) %all-to-all-start.1) | async-done | bytes 1056 | tf_op jit(solution)/shard_map/all_to_all | solution.py:47
  33.0 3.2 %all-to-all-start = ((s32[4,1,64]{2,1,0:T(1,128)}), s32[4,1,64]{2,1,0:T(1,128)S(1)}, u32[]{:S(2)}, u32[]{:S(2)}) async-start(s32[4,1,64]{2,1,0:T(1,128)} %all_to_all.19), calls=%async_computation | async-start | bytes 4096 | tf_op jit(solution)/shard_map/all_to_all | solution.py:46
  36.2 0.1 reshape.61
  36.3 0.5 broadcast.65
  36.8 0.7 reduce.13
  37.5 0.1 reshape.103
  37.5 2.7 %all-to-all-done = s32[4,1,64]{2,1,0:T(1,128)S(1)} async-done(((s32[4,1,64]{2,1,0:T(1,128)}), s32[4,1,64]{2,1,0:T(1,128)S(1)}, u32[]{:S(2)}, u32[]{:S(2)}) %all-to-all-start) | async-done | bytes 1056 | tf_op jit(solution)/shard_map/all_to_all | solution.py:46
  40.3 0.7 reduce.14
  40.9 0.1 eq.33
  41.0 0.1 reshape.101
  41.1 51.6 %all-gather.1 = s32[64,1,256]{2,1,0:T(1,128)S(1)} all-gather(s32[1,1,256]{2,1,0:T(1,128)S(1)} %reshape.103), channel_id=1, replica_groups=mesh['grp'=4,'blk'=64] {'blk'}, dimensions={0}, use_global_device_ids=true | all-gather | bytes 66560 | tf_op jit(solution)/shard_map/all_gather | solution.py:55
  92.7 42.7 %all-gather = s32[64,1,256]{2,1,0:T(1,128)S(1)} all-gather(s32[1,1,256]{2,1,0:T(1,128)S(1)} %reshape.101), channel_id=1, replica_groups=mesh['grp'=4,'blk'=64] {'blk'}, dimensions={0}, use_global_device_ids=true | all-gather | bytes 66560 | tf_op jit(solution)/shard_map/all_gather | solution.py:54
  135.4 34.9 %all-gather.4.cloned.1.call-done = bf16[16384,1024]{1,0:T(8,128)(2,1)} async-done(((bf16[256,1024]{1,0:T(8,128)(2,1)}), bf16[16384,1024]{1,0:T(8,128)(2,1)}) %all-gather.4.cloned.1.call-update) | async-done | bytes 33554448 | tf_op jit(solution)/shard_map/all_gather | solution.py:53
  170.3 16.4 %fusion = f32[256]{0:T(256)S(1)} fusion(bf16[256,1024]{1,0:T(8,128)(2,1)} %bitcast.9, bf16[16384,1024]{1,0:T(8,128)(2,1)} %all-gather.4.cloned.1.call-done, s32[256]{0:T(256)S(1)} %reshape.61, s32[16384]{0:T(1024)S(1)} %bitcast.11, pred[256]{0:T(512)(128)(4,1)S(1)} %broadcast_compare_fusion, s32[16384]{0:T(1024)S(1)} %bitcast.12, s32[256]{0:T(256)S(1)} %eq.33), kind=kOutput, calls=%fused_computation.5 | convolution fusion | flops 8615100416 | bytes 34213120 | tf_op jit(solution)/shard_map/dot_general | solution.py:15
  186.7 0.7 max_broadcast_in_dim.15
  187.4 4.0 %all-to-all-start.3 = ((f32[4,1,64]{2,1,0:T(1,128)}), f32[4,1,64]{2,1,0:T(1,128)S(1)}, u32[]{:S(2)}, u32[]{:S(2)}) async-start(f32[4,1,64]{2,1,0:T(1,128)} %max_broadcast_in_dim.15), calls=%async_computation.3 | async-start | bytes 4096 | tf_op jit(solution)/shard_map/all_to_all | solution.py:60
  191.4 4.1 %all-to-all-done.3 = f32[4,1,64]{2,1,0:T(1,128)S(1)} async-done(((f32[4,1,64]{2,1,0:T(1,128)}), f32[4,1,64]{2,1,0:T(1,128)S(1)}, u32[]{:S(2)}, u32[]{:S(2)}) %all-to-all-start.3) | async-done | bytes 1056 | tf_op jit(solution)/shard_map/all_to_all | solution.py:60
  195.5 0.5 broadcast.67
  196.0 0.7 reduce.15
  196.7 0.1 reshape.64
  196.7 1.8 gather_fusion
  (4 shorter events, 0.0 us)
Async XLA Ops:
  6.5 163.8 %all-gather.4.cloned.1.call-start = ((), (), s32[]{:S(2)}) async-start(), calls=%async_computation.4 | async-start | bytes 34078720 | tf_op jit(solution)/shard_map/all_gather | solution.py:53
  25.7 7.3 %all-to-all-start.1 = ((s32[4,1,64]{2,1,0:T(1,128)}), s32[4,1,64]{2,1,0:T(1,128)S(1)}, u32[]{:S(2)}, u32[]{:S(2)}) async-start(s32[4,1,64]{2,1,0:T(1,128)} %all_to_all.21), calls=%async_computation.1 | async-start | bytes 4096 | tf_op jit(solution)/shard_map/all_to_all | solution.py:47
  33.0 7.3 %all-to-all-start = ((s32[4,1,64]{2,1,0:T(1,128)}), s32[4,1,64]{2,1,0:T(1,128)S(1)}, u32[]{:S(2)}, u32[]{:S(2)}) async-start(s32[4,1,64]{2,1,0:T(1,128)} %all_to_all.19), calls=%async_computation | async-start | bytes 4096 | tf_op jit(solution)/shard_map/all_to_all | solution.py:46
  187.4 8.1 %all-to-all-start.3 = ((f32[4,1,64]{2,1,0:T(1,128)}), f32[4,1,64]{2,1,0:T(1,128)S(1)}, u32[]{:S(2)}, u32[]{:S(2)}) async-start(f32[4,1,64]{2,1,0:T(1,128)} %max_broadcast_in_dim.15), calls=%async_computation.3 | async-start | bytes 4096 | tf_op jit(solution)/shard_map/all_to_all | solution.py:60
Sparse Core Ops, SparseCore 0:
  24.0 146.2 all-gather.3
where the time goes:
time: 206 us; the launch traced here: 205 us
  blocking collectives  107 us (52%)
  waiting for transfers between devices  44 us (21%)
  matrix products  16.4 us (8%)
  between operations  13.5 us (7%)
  starting transfers between devices  10.4 us (5%)
  local copies, waits for them, and re-layouts  7.43 us (4%)
  other arithmetic  6.65 us (3%)
    all_gather x1, blocking collectives, shards(): piece_order = lax.all_gather(local_order, 'blk', axis=0, tiled=True)  51.6 us
    all_gather x1, blocking collectives, shards(): piece_cluster = lax.all_gather(local_cluster, 'blk', axis=0, tiled=True)  42.7 us
    all_gather x1, waiting for transfers between devices, shards(): piece_unit = lax.all_gather(local_unit, 'blk', axis=0, tiled=True)  34.9 us
    dot_general x1, matrix products, pair_scores(): lax.dot_general(left, right, (((1,), (1,)), ((), ())), preferred_element_...  16.4 us
    all_to_all x1, blocking collectives, shards(): lax.all_to_all(send_unit, 'grp', split_axis=0, concat_axis=0, tiled=True)  12.7 us
  transfers between devices with their start and end apart: 4, of which 4 were waited for; matrix products, arithmetic and copies ran while one was open for 2% of the time, Pallas kernels for 0%

commit v1 on v0

v1 whole, which is shorter than its diff:
```python
import functools
import jax
import jax.numpy as jnp
from jax import lax
from jax.experimental import pallas as pl
from jax.experimental.pallas import tpu as pltpu
from jax.sharding import PartitionSpec as P

MESH = pl.DeviceIdType.MESH
NX, NY, NZ = 4, 4, 8
CHUNKS = 65
HALF = ((0, 32), (32, 33))
OFF = (0, -1, 1, 2)
ZOFF = (0, -1, 1, -2, 2, -3, 3, 4)


def slot_c(a, b):
    return OFF.index(a) * 4 + OFF.index(b)


def wide(ref, start, count):
    value = ref[pl.ds(start, count), 0:64]
    return jnp.concatenate([value[:, k * 8:(k + 1) * 8].reshape(count * 128, 128) for k in range(8)], axis=1)


def keys_of(tag):
    tag = tag.astype(jnp.float32)
    low = tag[0:1] * 32768.0
    return low, low + tag[1:2] * 256.0 + tag[2:3]


def kernel(emb_ref, cid_ref, ord_ref, out_ref, C, R, keycol, qk, acc, res, send_sems, fsem, zsem, bsem, rsem):
    x = lax.axis_index("grp")
    blk = lax.axis_index("blk")
    core = lax.rem(blk, 2)
    y = lax.rem(lax.div(blk, 2), NY)
    z = lax.div(blk, 2 * NY)

    def dev(dx, dy, dz, dc):
        cc = lax.rem(core + dc, 2)
        return (lax.rem(x + dx, NX), (lax.rem(z + dz, NZ) * NY + lax.rem(y + dy, NY)) * 2 + cc)

    def first(d):
        d = d % 4
        return dev((1 - core) * d, core * d, 0, 0)

    def second(d):
        d = d % 4
        return dev(core * d, (1 - core) * d, 0, 0)

    def zdev(d):
        return dev(0, 0, d % NZ, 0)

    sib = dev(0, 0, 0, 1)

    barrier = pltpu.get_barrier_semaphore()
    for t in (first(1), first(-1), second(1), second(-1), zdev(1), zdev(-1), sib):
        pl.semaphore_signal(barrier, inc=1, device_id=t, device_id_type=MESH)

    values = emb_ref[...].astype(jnp.float32)
    total = jnp.sum(values * values, axis=1, keepdims=True)
    unit = (values * lax.rsqrt(total + 1e-06)).astype(jnp.bfloat16)
    for k in range(8):
        piece = unit[:, k * 128:(k + 1) * 128].reshape(8, 16, 128)
        C[0, k * 8:(k + 1) * 8] = piece
        R[0, k * 8:(k + 1) * 8] = piece
    row = lax.broadcasted_iota(jnp.int32, (16, 128), 0)
    order = ord_ref[...]
    tag = jnp.where(row == 0, cid_ref[...], jnp.where(row == 1, lax.shift_right_logical(order, 8), jnp.where(row == 2, order & 255, 0)))
    tag = tag.astype(jnp.float32).astype(jnp.bfloat16)
    C[0, 64] = tag
    R[0, 64] = tag
    pl.semaphore_wait(barrier, 7)

    sends = []

    def send(src, dst, sem, target):
        d = pltpu.make_async_remote_copy(src_ref=src, dst_ref=dst, send_sem=send_sems.at[len(sends)], recv_sem=sem, device_id=target, device_id_type=MESH)
        d.start()
        sends.append(d)

    def cpart(i, h):
        return C.at[i, pl.ds(*HALF[h])]

    def rpart(i, h):
        return R.at[i, pl.ds(*HALF[h])]

    def send_c(a, b, h, target):
        i, j = slot_c(*a), slot_c(*b)
        send(cpart(i, h), cpart(j, h), fsem.at[j, h], target)

    def wait_c(a, h):
        j = slot_c(*a)
        pltpu.make_async_remote_copy(src_ref=cpart(j, h), dst_ref=cpart(j, h), send_sem=send_sems.at[0], recv_sem=fsem.at[j, h], device_id=sib, device_id_type=MESH).wait_recv()

    def send_z(i, j, h, d):
        i, j = 2 * ZOFF.index(i), 2 * ZOFF.index(j)
        send(rpart(i, h), rpart(j, h), zsem.at[j // 2, h], zdev(d))

    def wait_z(k, h):
        j = 2 * ZOFF.index(k)
        pltpu.make_async_remote_copy(src_ref=rpart(j, h), dst_ref=rpart(j, h), send_sem=send_sems.at[0], recv_sem=zsem.at[j // 2, h], device_id=sib, device_id_type=MESH).wait_recv()

    def send_sib(k):
        j = 2 * ZOFF.index(k)
        send(R.at[j], R.at[j + 1], bsem.at[j // 2], sib)

    def wait_sib(k):
        j = 2 * ZOFF.index(k)
        pltpu.make_async_remote_copy(src_ref=R.at[j + 1], dst_ref=R.at[j + 1], send_sem=send_sems.at[0], recv_sem=bsem.at[j // 2], device_id=sib, device_id_type=MESH).wait_recv()

    def line(a, h):
        send_c((a, 0), (a, -1), h, second(1))
        send_c((a, 0), (a, 1), h, second(-1))

    def got_f(a, h):
        wait_c((a, 0), h)
        if (a, h) == (-1, 0):
            send_c((-1, 0), (2, 0), 0, first(1))
        if (a, h) == (1, 1):
            send_c((1, 0), (2, 0), 1, first(-1))
        line(a, h)

    def got_s(a, b, h):
        wait_c((a, b), h)
        if (b, h) == (-1, 0):
            send_c((a, -1), (a, 2), 0, second(1))
        if (b, h) == (1, 1):
            send_c((a, 1), (a, 2), 1, second(-1))

    def got_z(k, h):
        wait_z(k, h)
        if k < 0 and (k > -3 or h == 0):
            send_z(k, k - 1 if k > -3 else 4, h, 1)
        if 0 < k < 4 and (k < 3 or h == 1):
            send_z(k, k + 1, h, -1)

    def ready_r(k):
        wait_sib(k)
        u = ZOFF.index(k)
        for c in range(2):
            low, high = keys_of(R[2 * u + c, 64])
            qk[u, 0:1, c * 128:(c + 1) * 128] = low
            qk[u, 1:2, c * 128:(c + 1) * 128] = high

    def ready_c(start, count):
        def one(j, carry):
            _, high = keys_of(C[j, 64])
            keycol[j] = jnp.broadcast_to(high, (128, 128)).T
            return carry

        lax.fori_loop(start, start + count, one, 0)

    def compute(start, count, u0, u1):
        def one(u, carry):
            scores = lax.dot_general(
                wide(C, start, count), wide(R, 2 * u, 2), (((1,), (1,)), ((), ())),
                preferred_element_type=jnp.float32,
            )
            column = keycol[pl.ds(start, count)].reshape(count * 128, 128)
            column = jnp.concatenate([column, column], axis=1)
            mask = (column >= qk[u, 0:1, :]) & (column < qk[u, 1:2, :])
            kept = jnp.where(mask, scores, jnp.float32(-1.0))
            best = jnp.max(kept.reshape(count * 16, 8, 256), axis=0)
            acc[2 * u] = jnp.maximum(acc[2 * u], best[:, 0:128])
            acc[2 * u + 1] = jnp.maximum(acc[2 * u + 1], best[:, 128:256])
            return carry

        lax.fori_loop(u0, u1, one, 0)

    send_c((0, 0), (-1, 0), 0, first(1))
    send_c((0, 0), (1, 0), 1, first(-1))
    send_z(0, -1, 0, 1)
    send_z(0, 1, 1, -1)
    send_c((0, 0), (-1, 0), 1, first(1))
    send_c((0, 0), (1, 0), 0, first(-1))
    send_z(0, -1, 1, 1)
    send_z(0, 1, 0, -1)
    send_sib(0)
    acc[...] = jnp.full(acc.shape, -1.0, jnp.float32)
    sends[0].wait_send()
    sends[1].wait_send()
    line(0, 0)
    line(0, 1)

    got_f(-1, 0); got_f(1, 1)
    got_f(-1, 1); got_f(1, 0)
    got_z(-1, 0); got_z(1, 1)
    got_s(0, -1, 0); got_s(0, 1, 1)
    got_z(-1, 1); got_z(1, 0)
    send_sib(-1); send_sib(1)
    got_f(2, 0); got_f(2, 1)
    got_s(0, -1, 1); got_s(0, 1, 0)
    got_s(-1, -1, 0); got_s(-1, 1, 1)
    got_s(-1, -1, 1); got_s(-1, 1, 0)
    got_z(-2, 0); got_z(2, 1)
    got_s(0, 2, 0); got_s(0, 2, 1)
    ready_r(0); ready_r(-1); ready_r(1)
    ready_c(0, 4)
    compute(0, 4, 0, 3)
    got_s(1, -1, 0); got_s(1, 1, 1)
    got_s(1, -1, 1); got_s(1, 1, 0)
    got_z(-2, 1); got_z(2, 0)
    send_sib(-2); send_sib(2)
    got_s(-1, 2, 0); got_s(-1, 2, 1)
    ready_c(4, 4)
    compute(4, 4, 0, 3)
    got_z(-3, 0); got_z(3, 1)
    got_s(2, -1, 0); got_s(2, 1, 1)
    got_s(1, 2, 0); got_s(1, 2, 1)
    ready_r(-2); ready_r(2)
    compute(0, 8, 3, 5)
    got_z(-3, 1); got_z(3, 0)
    send_sib(-3); send_sib(3)
    ready_c(8, 4)
    compute(8, 4, 0, 5)
    got_s(2, -1, 1); got_s(2, 1, 0)
    ready_r(-3); ready_r(3)
    compute(0, 12, 5, 7)
    got_z(4, 0); got_z(4, 1)
    send_sib(4)
    got_s(2, 2, 0); got_s(2, 2, 1)
    ready_c(12, 4)
    compute(12, 4, 0, 7)
    ready_r(4)
    compute(0, 16, 7, 8)

    waits = []
    for k in ZOFF:
        for c in range(2):
            if (k, c) == (0, 0):
                continue
            i = 2 * ZOFF.index(k) + c
            j = 2 * ZOFF.index(-k if k != 4 else 4) + c
            d = pltpu.make_async_remote_copy(
                src_ref=acc.at[i], dst_ref=res.at[j], send_sem=send_sems.at[len(sends)], recv_sem=rsem.at[j],
                device_id=dev(0, 0, k % NZ, c), device_id_type=MESH,
            )
            d.start()
            sends.append(d)
            waits.append(j)
    for d in sends[2:]:
        d.wait_send()
    best = acc[0]
    for j in waits:
        pltpu.make_async_remote_copy(
            src_ref=res.at[j], dst_ref=res.at[j], send_sem=send_sems.at[0], recv_sem=rsem.at[j],
            device_id=sib, device_id_type=MESH,
        ).wait_recv()
        best = jnp.maximum(best, res[j])
    out_ref[...] = jnp.max(best, axis=0, keepdims=True)


def shards(embeddings, cluster_ids, row_order):
    out = pl.pallas_call(
        kernel,
        out_shape=jax.ShapeDtypeStruct((1, 128), jnp.float32),
        in_specs=[pl.BlockSpec(memory_space=pltpu.VMEM)] * 3,
        out_specs=pl.BlockSpec(memory_space=pltpu.VMEM),
        scratch_shapes=[
            pltpu.VMEM((16, CHUNKS, 16, 128), jnp.bfloat16),
            pltpu.VMEM((16, CHUNKS, 16, 128), jnp.bfloat16),
            pltpu.VMEM((16, 128, 128), jnp.float32),
            pltpu.VMEM((8, 8, 256), jnp.float32),
            pltpu.VMEM((16, 8, 128), jnp.float32),
            pltpu.VMEM((16, 8, 128), jnp.float32),
            pltpu.SemaphoreType.DMA((96,)),
            pltpu.SemaphoreType.DMA((16, 2)),
            pltpu.SemaphoreType.DMA((8, 2)),
            pltpu.SemaphoreType.DMA((8,)),
            pltpu.SemaphoreType.DMA((16,)),
        ],
        compiler_params=pltpu.CompilerParams(collective_id=0, has_side_effects=True, vmem_limit_bytes=48 << 20),
        name="gather_all",
    )(embeddings, cluster_ids.reshape(1, 128), row_order.reshape(1, 128))
    return out.reshape(128)


def solution(mesh):
    in_specs = (P(("grp", "blk"), None), P(("grp", "blk")), P(("grp", "blk")))
    return jax.shard_map(shards, mesh=mesh, in_specs=in_specs, out_specs=P(("grp", "blk")), check_vma=False)
```

time: 206 us -> 53.4 us (0.26)
  blocking collectives: 107 us -> 0 us
  Pallas kernels: 0 us -> 51.1 us
  waiting for transfers between devices: 44 us -> 0 us
  matrix products: 16.4 us -> 0 us
  between operations: 13.5 us -> 0.01 us
  starting transfers between devices: 10.4 us -> 0 us
  other arithmetic: 6.65 us -> 0 us
  local copies, waits for them, and re-layouts: 7.43 us -> 2.13 us
    all_gather x2 -> x0, blocking collectives: 94.3 us -> none  [the longest x1 51.6 us: shards(): piece_order = lax.all_gather(local_order, 'blk', axis=0, tiled=True)]
    pallas_call x0 -> x1, Pallas kernels: none -> 51.1 us  [shards(): pl.pallas_call(kernel, out_shape=jax.ShapeDtypeStruct((1, 128), jnp.float...]
    all_gather x1 -> x0, waiting for transfers between devices: 34.9 us -> none  [shards(): piece_unit = lax.all_gather(local_unit, 'blk', axis=0, tiled=True)]
    dot_general x1 -> x0, matrix products: 16.4 us -> none  [pair_scores(): lax.dot_general(left, right, (((1,), (1,)), ((), ())), preferred_element_...]
    all_to_all x1 -> x0, blocking collectives: 12.7 us -> none  [shards(): lax.all_to_all(send_unit, 'grp', split_axis=0, concat_axis=0, tiled=True)]
    all_to_all x3 -> x0, starting transfers between devices: 10.4 us -> none  [the longest x1 3.97 us: shards(): lax.all_to_all(best.reshape(groups, capacity), 'grp', split_axis=0, conca...]
    all_to_all x3 -> x0, waiting for transfers between devices: 9.12 us -> none  [the longest x1 4.1 us: shards(): lax.all_to_all(best.reshape(groups, capacity), 'grp', split_axis=0, conca...]
    all_to_all x4 -> x0, local copies, waits for them, and re-layouts: 2.36 us -> none  [the longest x2 1.18 us: shards(): lax.all_to_all(send_order, 'grp', split_axis=0, concat_axis=0, tiled=True)]
  transfers between devices with their start and end apart: 4 -> 0, of which waited for: 4 -> 0; matrix products, arithmetic and copies ran while one was open for 2% -> 0% of each run, Pallas kernels for 0% -> 0%
where the time goes in v1:
time: 53.4 us; the launch traced here: 53.2 us
  Pallas kernels  51.1 us (96%)
  local copies, waits for them, and re-layouts  2.13 us (4%)
    pallas_call x1, Pallas kernels, shards(): pl.pallas_call(kernel, out_shape=jax.ShapeDtypeStruct((1, 128), jnp.float...  51.1 us
    unnamed x7, local copies, waits for them, and re-layouts  2.13 us

profile of v1, /device:TPU:1, one launch (start us, length us, event | category | flops | bytes accessed | tf_op | source)
XLA Modules:
  0.0 53.2 jit_solution(12270943092162640634)
XLA Ops:
  0.0 0.0 copy-start.1
  0.0 0.0 copy-start.2
  0.0 0.7 %copy-done.1 = s32[128]{0:T(128)S(1)} copy-done((s32[128]{0:T(128)S(1)}, s32[128]{0:T(128)}, u32[]{:S(2)}) %copy-start.1) | copy-done | bytes 536
  0.7 0.0 copy-done.2
  0.7 0.0 copy-start
  0.7 0.9 %copy-done = bf16[128,1024]{1,0:T(8,128)(2,1)S(1)} copy-done((bf16[128,1024]{1,0:T(8,128)(2,1)S(1)}, bf16[128,1024]{1,0:T(8,128)(2,1)}, u32[]{:S(2)}) %copy-start) | copy-done | bytes 262168
  1.6 51.1 %gather_all.1 = f32[1,128]{1,0:T(1,128)S(1)} custom-call(bf16[128,1024]{1,0:T(8,128)(2,1)S(1)} %copy-done, s32[1,128]{1,0:T(1,128)S(1)} %bitcast.3, s32[1,128]{1,0:T(1,128)S(1)} %bitcast.4), custom_call_target="tpu_custom_call" | custom-call | tf_op jit(solution)/shard_map/gather_all/pallas_call | solution.py:255
  52.7 0.5 copy.5
Async XLA Ops:
  0.0 0.7 %copy-start.1 = (s32[128]{0:T(128)S(1)}, s32[128]{0:T(128)}, u32[]{:S(2)}) copy-start(s32[128]{0:T(128)} %param.4) | copy-start | bytes 1540
  0.0 0.7 %copy-start.2 = (s32[128]{0:T(128)S(1)}, s32[128]{0:T(128)}, u32[]{:S(2)}) copy-start(s32[128]{0:T(128)} %param.5) | copy-start | bytes 1540
  0.7 0.9 %copy-start = (bf16[128,1024]{1,0:T(8,128)(2,1)S(1)}, bf16[128,1024]{1,0:T(8,128)(2,1)}, u32[]{:S(2)}) copy-start(bf16[128,1024]{1,0:T(8,128)(2,1)} %emb_ref.1) | copy-start | bytes 786436

commit v2 on v0

v2 whole, which is shorter than its diff:
```python
import functools
import jax
import jax.numpy as jnp
from jax import lax
from jax.experimental import pallas as pl
from jax.experimental.pallas import tpu as pltpu
from jax.sharding import PartitionSpec as P

MESH = pl.DeviceIdType.MESH
NX, NY, NZ = 4, 4, 8
CHUNKS = 65
HALVES = ((0, 32), (32, 33))
QUARTERS = ((0, 16), (16, 16), (32, 16), (48, 17))
PLANE = ((0, 0), (1, 0), (0, 1), (3, 3), (2, 0), (0, 2), (2, 3), (3, 2), (1, 3), (2, 2))
COLUMN = (0, -1, 1, -2, 2, -3, 3, 4)

def wide(ref, start, count):
    value = ref[pl.ds(start, count), 0:64]
    return jnp.concatenate([value[:, k * 8:(k + 1) * 8].reshape(count * 128, 128) for k in range(8)], axis=1)


def keys_of(tag):
    tag = tag.astype(jnp.float32)
    low = tag[0:1] * 32768.0
    return low, low + tag[1:2] * 256.0 + tag[2:3]


def kernel(emb_ref, cid_ref, ord_ref, out_ref, C, R, keycol, qk, acc_r, acc_c, out_c, res_r, res_c, send_sems, csem, zsem, bsem, rsem_r, rsem_c):
    x = lax.axis_index("grp")
    blk = lax.axis_index("blk")
    core = lax.rem(blk, 2)
    y = lax.rem(lax.div(blk, 2), NY)
    z = lax.div(blk, 2 * NY)

    def dev(dx, dy, dz, dc):
        other = lax.rem(core + dc, 2)
        return (lax.rem(x + dx % NX, NX), (lax.rem(z + dz % NZ, NZ) * NY + lax.rem(y + dy % NY, NY)) * 2 + other)

    sib = dev(0, 0, 0, 1)

    barrier = pltpu.get_barrier_semaphore()
    near = [dev(1, 0, 0, 0), dev(-1, 0, 0, 0), dev(0, 1, 0, 0), dev(0, -1, 0, 0), dev(1, 1, 0, 0), dev(-1, -1, 0, 0), dev(0, 0, 1, 0), dev(0, 0, -1, 0), sib]
    for target in near:
        pl.semaphore_signal(barrier, inc=1, device_id=target, device_id_type=MESH)

    values = emb_ref[...].astype(jnp.float32)
    total = jnp.sum(values * values, axis=1, keepdims=True)
    unit = (values * lax.rsqrt(total + 1e-06)).astype(jnp.bfloat16)
    for k in range(8):
        piece = unit[:, k * 128:(k + 1) * 128].reshape(8, 16, 128)
        C[0, k * 8:(k + 1) * 8] = piece
        R[0, k * 8:(k + 1) * 8] = piece
    row = lax.broadcasted_iota(jnp.int32, (16, 128), 0)
    order = ord_ref[...]
    tag = jnp.where(row == 0, cid_ref[...], jnp.where(row == 1, lax.shift_right_logical(order, 8), jnp.where(row == 2, order & 255, 0)))
    tag = tag.astype(jnp.float32).astype(jnp.bfloat16)
    C[0, 64] = tag
    R[0, 64] = tag
    pl.semaphore_wait(barrier, len(near))

    sends = []

    def copy(src, dst, sem, target):
        d = pltpu.make_async_remote_copy(
            src_ref=src, dst_ref=dst, send_sem=send_sems.at[len(sends)], recv_sem=sem, device_id=target, device_id_type=MESH
        )
        d.start()
        sends.append(d)

    def arrived(dst, sem):
        pltpu.make_async_remote_copy(
            src_ref=dst, dst_ref=dst, send_sem=send_sems.at[0], recv_sem=sem, device_id=sib, device_id_type=MESH
        ).wait_recv()

    def cpart(j, h):
        return C.at[j, pl.ds(*HALVES[h])]

    def zpart(u, q):
        return R.at[2 * u, pl.ds(*QUARTERS[q])]

    def pass_c(d, step, h):
        i = PLANE.index(d)
        j = PLANE.index(((d[0] - step[0]) % NX, (d[1] - step[1]) % NY))
        copy(cpart(i, h), cpart(j, h), csem.at[j, h], dev(step[0], step[1], 0, 0))

    def got_c(d, h):
        j = PLANE.index(d)
        arrived(cpart(j, h), csem.at[j, h])

    def pass_z(k, q, steps=(1, -1)):
        i = COLUMN.index(k)
        for step in steps:
            if k * step > 0 or k == 4 or (abs(k) == 3 and q // 2 != (step + 1) // 2):
                continue
            to = k - step
            j = COLUMN.index(4 if abs(to) == 4 else to)
            copy(zpart(i, q), zpart(j, q), zsem.at[j, q], dev(0, 0, step, 0))

    def got_z(k, q):
        j = COLUMN.index(k)
        arrived(zpart(j, q), zsem.at[j, q])
        if k != 4:
            pass_z(k, q)

    def step_z(k, n):
        got_z(-k, (n + 2) % 4)
        got_z(k, n)

    def share(k):
        u = COLUMN.index(k)
        copy(R.at[2 * u], R.at[2 * u + 1], bsem.at[u], sib)

    def ready_r(k):
        u = COLUMN.index(k)
        arrived(R.at[2 * u + 1], bsem.at[u])
        for c in range(2):
            low, high = keys_of(R[2 * u + c, 64])
            qk[u, 0:1, c * 128:(c + 1) * 128] = low
            qk[u, 1:2, c * 128:(c + 1) * 128] = high

    def ready_c(start, count):
        def one(j, carry):
            _, high = keys_of(C[j, 64])
            keycol[j] = jnp.broadcast_to(high, (128, 128)).T
            return carry

        lax.fori_loop(start, start + count, one, 0)

    def compute(start, count, u0, u1):
        def one(u, carry):
            scores = lax.dot_general(
                wide(C, start, count), wide(R, 2 * u, 2), (((1,), (1,)), ((), ())),
                preferred_element_type=jnp.float32,
            )
            column = keycol[pl.ds(start, count)].reshape(count * 128, 128)
            column = jnp.concatenate([column, column], axis=1)
            low = qk[u, 0:1, :]
            high = qk[u, 1:2, :]
            low_r = jnp.where((column >= low) & (column < high), scores, jnp.float32(-1.0))
            best = jnp.max(low_r.reshape(count * 16, 8, 256), axis=0)
            acc_r[2 * u] = jnp.maximum(acc_r[2 * u], best[:, 0:128])
            acc_r[2 * u + 1] = jnp.maximum(acc_r[2 * u + 1], best[:, 128:256])
            low_c = jnp.where((column > high) & (column < low + 32768.0), scores, jnp.float32(-1.0))
            side = jnp.maximum(low_c[:, 0:128], low_c[:, 128:256]).reshape(count, 128, 128)
            acc_c[pl.ds(start, count)] = jnp.maximum(acc_c[pl.ds(start, count)], side)
            return carry

        if u1 - u0 == 1:
            one(u0, 0)
        else:
            lax.fori_loop(u0, u1, one, 0)

    def answer_r(k):
        u = COLUMN.index(k)
        v = COLUMN.index(4 if k == 4 else -k)
        for c in range(2):
            if (k, c) != (0, 0):
                copy(acc_r.at[2 * u + c], res_r.at[2 * v + c], rsem_r.at[2 * v + c], dev(0, 0, k, c))

    for q in range(4):
        pass_z(0, (q + 2) % 4, (1,))
        pass_z(0, q, (-1,))
        if q % 2 == 0:
            h = q // 2
            pass_c((0, 0), (-1, 0), h)
            pass_c((0, 0), (0, -1), h)
            pass_c((0, 0), (1, 1), 1 - h)
    share(0)
    acc_r[...] = jnp.full(acc_r.shape, -1.0, jnp.float32)
    acc_c[...] = jnp.full(acc_c.shape, -1.0, jnp.float32)

    step_z(1, 0)
    step_z(1, 1)
    got_c((1, 0), 0)
    pass_c((1, 0), (-1, 0), 0)
    got_c((0, 1), 0)
    pass_c((0, 1), (0, -1), 0)
    got_c((3, 3), 1)
    pass_c((3, 3), (1, 0), 1)
    pass_c((3, 3), (0, 1), 1)
    step_z(1, 2)
    pass_c((1, 0), (0, 1), 0)
    step_z(1, 3)
    share(-1)
    share(1)
    got_c((1, 0), 1)
    pass_c((1, 0), (-1, 0), 1)
    got_c((0, 1), 1)
    pass_c((0, 1), (0, -1), 1)
    got_c((3, 3), 0)
    pass_c((3, 3), (1, 0), 0)
    pass_c((3, 3), (0, 1), 0)
    ready_r(0)
    ready_c(0, 4)
    step_z(2, 0)
    compute(0, 4, 0, 1)
    ready_r(-1)
    ready_r(1)
    step_z(2, 1)
    got_c((2, 3), 1)
    pass_c((2, 3), (1, 0), 1)
    got_c((3, 2), 1)
    pass_c((3, 2), (1, 0), 1)
    compute(0, 4, 1, 3)
    step_z(2, 2)
    step_z(2, 3)
    share(-2)
    share(2)
    got_c((2, 3), 0)
    pass_c((2, 3), (0, 1), 0)
    got_c((2, 0), 0)
    got_c((2, 0), 1)
    got_c((0, 2), 0)
    got_c((0, 2), 1)
    got_c((3, 2), 0)
    ready_c(4, 4)
    compute(4, 4, 0, 1)
    step_z(3, 0)
    compute(4, 4, 1, 3)
    step_z(3, 1)
    ready_r(-2)
    ready_r(2)
    compute(0, 8, 3, 4)
    step_z(3, 2)
    compute(0, 8, 4, 5)
    step_z(3, 3)
    share(-3)
    share(3)
    got_c((1, 3), 0)
    got_c((1, 3), 1)
    got_c((2, 2), 0)
    got_c((2, 2), 1)
    ready_c(8, 2)
    compute(8, 2, 0, 5)
    for k in (0, -1, 1, -2, 2):
        answer_r(k)
    for q in range(4):
        got_z(4, q)
    share(4)
    ready_r(-3)
    ready_r(3)
    compute(0, 10, 5, 7)
    answer_r(-3)
    answer_r(3)
    ready_r(4)
    compute(0, 10, 7, 8)
    answer_r(4)
    for j, d in enumerate(PLANE):
        out_c[j] = jnp.max(acc_c[j].T.reshape(16, 8, 128), axis=0)
        if j:
            copy(out_c.at[j], res_c.at[j], rsem_c.at[j], dev(d[0], d[1], 0, 0))

    best = jnp.maximum(acc_r[0], out_c[0])
    for j in range(1, 16):
        arrived(res_r.at[j], rsem_r.at[j])
        best = jnp.maximum(best, res_r[j])
    for j in range(1, 10):
        arrived(res_c.at[j], rsem_c.at[j])
        best = jnp.maximum(best, res_c[j])
    out_ref[...] = jnp.max(best, axis=0, keepdims=True)
    for d in sends:
        d.wait_send()


def shards(embeddings, cluster_ids, row_order):
    out = pl.pallas_call(
        kernel,
        out_shape=jax.ShapeDtypeStruct((1, 128), jnp.float32),
        in_specs=[pl.BlockSpec(memory_space=pltpu.VMEM)] * 3,
        out_specs=pl.BlockSpec(memory_space=pltpu.VMEM),
        scratch_shapes=[
            pltpu.VMEM((10, CHUNKS, 16, 128), jnp.bfloat16),
            pltpu.VMEM((16, CHUNKS, 16, 128), jnp.bfloat16),
            pltpu.VMEM((10, 128, 128), jnp.float32),
            pltpu.VMEM((8, 8, 256), jnp.float32),
            pltpu.VMEM((16, 8, 128), jnp.float32),
            pltpu.VMEM((10, 128, 128), jnp.float32),
            pltpu.VMEM((10, 8, 128), jnp.float32),
            pltpu.VMEM((16, 8, 128), jnp.float32),
            pltpu.VMEM((10, 8, 128), jnp.float32),
            pltpu.SemaphoreType.DMA((96,)),
            pltpu.SemaphoreType.DMA((10, 2)),
            pltpu.SemaphoreType.DMA((8, 4)),
            pltpu.SemaphoreType.DMA((8,)),
            pltpu.SemaphoreType.DMA((16,)),
            pltpu.SemaphoreType.DMA((10,)),
        ],
        compiler_params=pltpu.CompilerParams(collective_id=0, has_side_effects=True, vmem_limit_bytes=48 << 20),
        name="nearest_earlier",
    )(embeddings, cluster_ids.reshape(1, 128), row_order.reshape(1, 128))
    return out.reshape(128)


def solution(mesh):
    in_specs = (P(("grp", "blk"), None), P(("grp", "blk")), P(("grp", "blk")))
    return jax.shard_map(shards, mesh=mesh, in_specs=in_specs, out_specs=P(("grp", "blk")), check_vma=False)
```

time: 206 us -> 46.7 us (0.23)
  blocking collectives: 107 us -> 0 us
  Pallas kernels: 0 us -> 44.5 us
  waiting for transfers between devices: 44 us -> 0 us
  matrix products: 16.4 us -> 0 us
  between operations: 13.5 us -> 0.01 us
  starting transfers between devices: 10.4 us -> 0 us
  other arithmetic: 6.65 us -> 0 us
  local copies, waits for them, and re-layouts: 7.43 us -> 2.13 us
    all_gather x2 -> x0, blocking collectives: 94.3 us -> none  [the longest x1 51.6 us: shards(): piece_order = lax.all_gather(local_order, 'blk', axis=0, tiled=True)]
    pallas_call x0 -> x1, Pallas kernels: none -> 44.5 us  [shards(): pl.pallas_call(kernel, out_shape=jax.ShapeDtypeStruct((1, 128), jnp.float...]
    all_gather x1 -> x0, waiting for transfers between devices: 34.9 us -> none  [shards(): piece_unit = lax.all_gather(local_unit, 'blk', axis=0, tiled=True)]
    dot_general x1 -> x0, matrix products: 16.4 us -> none  [pair_scores(): lax.dot_general(left, right, (((1,), (1,)), ((), ())), preferred_element_...]
    all_to_all x1 -> x0, blocking collectives: 12.7 us -> none  [shards(): lax.all_to_all(send_unit, 'grp', split_axis=0, concat_axis=0, tiled=True)]
    all_to_all x3 -> x0, starting transfers between devices: 10.4 us -> none  [the longest x1 3.97 us: shards(): lax.all_to_all(best.reshape(groups, capacity), 'grp', split_axis=0, conca...]
    all_to_all x3 -> x0, waiting for transfers between devices: 9.12 us -> none  [the longest x1 4.1 us: shards(): lax.all_to_all(best.reshape(groups, capacity), 'grp', split_axis=0, conca...]
    all_to_all x4 -> x0, local copies, waits for them, and re-layouts: 2.36 us -> none  [the longest x2 1.18 us: shards(): lax.all_to_all(send_order, 'grp', split_axis=0, concat_axis=0, tiled=True)]
  transfers between devices with their start and end apart: 4 -> 0, of which waited for: 4 -> 0; matrix products, arithmetic and copies ran while one was open for 2% -> 0% of each run, Pallas kernels for 0% -> 0%
where the time goes in v2:
time: 46.7 us; the launch traced here: 46.6 us
  Pallas kernels  44.5 us (95%)
  local copies, waits for them, and re-layouts  2.13 us (5%)
    pallas_call x1, Pallas kernels, shards(): pl.pallas_call(kernel, out_shape=jax.ShapeDtypeStruct((1, 128), jnp.float...  44.5 us
    unnamed x7, local copies, waits for them, and re-layouts  2.13 us

profile of v2, /device:TPU:1, one launch (start us, length us, event | category | flops | bytes accessed | tf_op | source)
XLA Modules:
  0.0 46.6 jit_solution(241850410486468915)
XLA Ops:
  0.0 0.0 copy-start.1
  0.0 0.0 copy-start.2
  0.0 0.7 %copy-done.1 = s32[128]{0:T(128)S(1)} copy-done((s32[128]{0:T(128)S(1)}, s32[128]{0:T(128)}, u32[]{:S(2)}) %copy-start.1) | copy-done | bytes 536
  0.7 0.0 copy-done.2
  0.7 0.0 copy-start
  0.7 0.9 %copy-done = bf16[128,1024]{1,0:T(8,128)(2,1)S(1)} copy-done((bf16[128,1024]{1,0:T(8,128)(2,1)S(1)}, bf16[128,1024]{1,0:T(8,128)(2,1)}, u32[]{:S(2)}) %copy-start) | copy-done | bytes 262168
  1.6 44.5 %nearest_earlier.1 = f32[1,128]{1,0:T(1,128)S(1)} custom-call(bf16[128,1024]{1,0:T(8,128)(2,1)S(1)} %copy-done, s32[1,128]{1,0:T(1,128)S(1)} %bitcast.3, s32[1,128]{1,0:T(1,128)S(1)} %bitcast.4), custom_call_target="tpu_custom_call" | custom-call | tf_op jit(solution)/shard_map/nearest_earlier/pallas_call | solution.py:266
  46.1 0.5 %copy.5 = f32[128]{0:T(128)} copy(f32[128]{0:T(128)S(1)} %bitcast.5) | data formatting | bytes 1024
Async XLA Ops:
  0.0 0.7 %copy-start.1 = (s32[128]{0:T(128)S(1)}, s32[128]{0:T(128)}, u32[]{:S(2)}) copy-start(s32[128]{0:T(128)} %param.4) | copy-start | bytes 1540
  0.0 0.7 %copy-start.2 = (s32[128]{0:T(128)S(1)}, s32[128]{0:T(128)}, u32[]{:S(2)}) copy-start(s32[128]{0:T(128)} %param.5) | copy-start | bytes 1540
  0.7 0.9 %copy-start = (bf16[128,1024]{1,0:T(8,128)(2,1)S(1)}, bf16[128,1024]{1,0:T(8,128)(2,1)}, u32[]{:S(2)}) copy-start(bf16[128,1024]{1,0:T(8,128)(2,1)} %emb_ref.1) | copy-start | bytes 786436

commit v3 on v0

v3 whole, which is shorter than its diff:
```python
import jax
import jax.numpy as jnp
from jax import lax
from jax.experimental import pallas as pl
from jax.experimental.pallas import tpu as pltpu
from jax.sharding import PartitionSpec as P

MESH = pl.DeviceIdType.MESH
NX, NY, NZ = 4, 4, 8
CHUNKS = 65
HALVES = ((0, 33), (33, 32))
QUARTERS = ((0, 17), (17, 16), (33, 16), (49, 16))
EARLY, LATE = (0, 1, 4, 5), (2, 3, 6, 7)
PLANE = ((1, 0), (0, 1), (3, 3), (2, 3), (1, 3), (3, 2), (0, 0), (2, 0), (0, 2), (2, 2))
OWN = PLANE.index((0, 0))
COLUMN = (0, 1, -1, 2, -2, 3, -3, 4)
ONWARD = {
    (0, 0): (((-1, 0), (0, 1, 2, 3)), ((0, -1), (0, 1, 2, 3))),
    (1, 0): (((-1, 0), (0, 1, 2, 3)), ((0, 1), (0, 1))),
    (0, 1): (((0, -1), (0, 1, 2, 3)),),
    (3, 3): (((1, 0), (0, 1, 2, 3)), ((0, 1), (0, 1, 2, 3))),
    (2, 3): (((1, 0), (2, 3)), ((0, 1), (0, 1))),
    (3, 2): (((1, 0), (2, 3)),),
}


def wide(ref, start, count, features=range(8)):
    return jnp.concatenate(
        [ref[pl.ds(start, count), 1 + k * 8:9 + k * 8].reshape(count * 128, 128) for k in features], axis=1
    )


def product(left, right):
    return lax.dot_general(left, right, (((1,), (1,)), ((), ())), preferred_element_type=jnp.float32)


def keys_of(tag):
    tag = tag.astype(jnp.float32)
    low = tag[0:1] * 32768.0
    return low, low + tag[1:2] * 256.0 + tag[2:3]


def kernel(emb_hbm, cid_hbm, ord_hbm, out_ref, emb_ref, cid_ref, ord_ref, in_sems, C, R, row_key, low_key, high_key, half, acc_r, acc_c, out_r, res_r, res_c, send_sems, csem, ssem, zsem, rsem_r, rsem_c, corner_sem):
    loads = [
        pltpu.make_async_copy(src, dst, in_sems.at[i])
        for i, (src, dst) in enumerate(((emb_hbm, emb_ref), (cid_hbm, cid_ref), (ord_hbm, ord_ref)))
    ]
    for load in loads:
        load.start()
    x = lax.axis_index("grp")
    blk = lax.axis_index("blk")
    core = lax.rem(blk, 2)
    y = lax.rem(lax.div(blk, 2), NY)
    z = lax.div(blk, 2 * NY)

    def dev(dx, dy, dz, dc):
        other = lax.rem(core + dc, 2)
        return (lax.rem(x + dx % NX, NX), (lax.rem(z + dz % NZ, NZ) * NY + lax.rem(y + dy % NY, NY)) * 2 + other)

    sib = dev(0, 0, 0, 1)

    barrier = pltpu.get_barrier_semaphore()
    near = [dev(1, 0, 0, 0), dev(-1, 0, 0, 0), dev(0, 1, 0, 0), dev(0, -1, 0, 0), dev(0, 0, 1, 0), dev(0, 0, -1, 0), sib]
    for target in near:
        pl.semaphore_signal(barrier, inc=1, device_id=target, device_id_type=MESH)

    for load in loads:
        load.wait()
    values = emb_ref[...].astype(jnp.float32)
    total = jnp.sum(values * values, axis=1, keepdims=True)
    unit = (values * lax.rsqrt(total + 1e-06)).astype(jnp.bfloat16)
    for k in range(8):
        piece = unit[:, k * 128:(k + 1) * 128].reshape(8, 16, 128)
        C[2 * OWN, 1 + k * 8:9 + k * 8] = piece
        R[0, 1 + k * 8:9 + k * 8] = piece
    row = lax.broadcasted_iota(jnp.int32, (16, 128), 0)
    order = ord_ref[...]
    tag = jnp.where(row == 0, cid_ref[...], jnp.where(row == 1, lax.shift_right_logical(order, 8), jnp.where(row == 2, order & 255, 0)))
    tag = tag.astype(jnp.float32).astype(jnp.bfloat16)
    C[2 * OWN, 0] = tag
    R[0, 0] = tag
    pl.semaphore_wait(barrier, len(near))

    sends = []

    def copy(src, dst, sem, target):
        d = pltpu.make_async_remote_copy(
            src_ref=src, dst_ref=dst, send_sem=send_sems.at[len(sends)], recv_sem=sem, device_id=target, device_id_type=MESH
        )
        d.start()
        sends.append(d)

    def arrived(dst, sem):
        pltpu.make_async_remote_copy(
            src_ref=dst, dst_ref=dst, send_sem=send_sems.at[0], recv_sem=sem, device_id=sib, device_id_type=MESH
        ).wait_recv()

    def cpart(i, q):
        return C.at[2 * i, pl.ds(*QUARTERS[q])]

    def zpart(u, q):
        return R.at[u, pl.ds(*QUARTERS[q])]

    def pass_c(d, step, q):
        i = PLANE.index(d)
        j = PLANE.index(((d[0] - step[0]) % NX, (d[1] - step[1]) % NY))
        copy(cpart(i, q), cpart(j, q), csem.at[j, q], dev(step[0], step[1], 0, 0))

    def share(i, h):
        copy(C.at[2 * i, pl.ds(*HALVES[h])], C.at[2 * i + 1, pl.ds(*HALVES[h])], ssem.at[i, h], sib)

    def got_c(d, *quarters):
        i = PLANE.index(d)
        for q in quarters:
            arrived(cpart(i, q), csem.at[i, q])
            for step, some in ONWARD.get(d, ()):
                if q in some:
                    pass_c(d, step, q)
            if q % 2:
                share(i, q // 2)

    def pass_z(k, q, steps=(1, -1)):
        i = COLUMN.index(k)
        for step in steps:
            if k * step > 0 or (abs(k) == 3 and q // 2 != (step + 1) // 2):
                continue
            to = k - step
            j = COLUMN.index(4 if abs(to) == 4 else to)
            copy(zpart(i, q), zpart(j, q), zsem.at[j, q], dev(0, 0, step, 0))

    def got_z(k, q):
        j = COLUMN.index(k)
        arrived(zpart(j, q), zsem.at[j, q])
        if k != 4:
            pass_z(k, q)

    def step_z(k, n):
        got_z(-k, (n + 2) % 4)
        got_z(k, n)

    def ready_c(start, count):
        for i in range(start, start + count):
            for h in range(2):
                arrived(C.at[2 * i + 1, pl.ds(*HALVES[h])], ssem.at[i, h])
            for j in (2 * i, 2 * i + 1):
                low, high = keys_of(C[j, 0])
                low_key[j, 0:1, :] = low
                high_key[j, 0:1, :] = high

    def ready_r(*ks):
        for k in ks:
            u = COLUMN.index(k)
            _, high = keys_of(R[u, 0])
            row_key[u] = jnp.broadcast_to(high, (128, 128)).T

    def use(scores, start, count, ks):
        for a, k in enumerate(ks):
            u = COLUMN.index(k)
            key = row_key[u]
            side = acc_r[u]
            for b in range(2 * count):
                j = 2 * start + b
                part = scores[a * 128:(a + 1) * 128, b * 128:(b + 1) * 128]
                low = low_key[j, 0:1, :]
                high = high_key[j, 0:1, :]
                earlier = jnp.where((key >= low) & (key < high), part, jnp.float32(-1.0))
                acc_c[j] = jnp.maximum(acc_c[j], jnp.max(earlier.reshape(16, 8, 128), axis=0))
                side = jnp.maximum(side, jnp.where((key > high) & (key < low + 32768.0), part, jnp.float32(-1.0)))
            acc_r[u] = side

    def compute(start, count, *ks):
        rows = jnp.concatenate([wide(R, COLUMN.index(k), 1) for k in ks], axis=0)
        use(product(rows, wide(C, 2 * start, 2 * count)), start, count, ks)

    def answer_r(*ks):
        for k in ks:
            u = COLUMN.index(k)
            out_r[u] = jnp.max(acc_r[u].T.reshape(16, 8, 128), axis=0)
            if k:
                v = COLUMN.index(4 if k == 4 else -k)
                copy(out_r.at[u], res_r.at[v], rsem_r.at[v], dev(0, 0, k, 0))

    def answer_c(*blocks):
        for i in blocks:
            for c in range(2):
                j = 2 * i + c
                if j != 2 * OWN:
                    copy(acc_c.at[j], res_c.at[j], rsem_c.at[j], dev(PLANE[i][0], PLANE[i][1], 0, c))

    pl.semaphore_signal(corner_sem, inc=1, device_id=dev(-1, 0, 0, 0), device_id_type=MESH)

    for q in range(4):
        pass_z(0, (q + 2) % 4, (1,))
        pass_z(0, q, (-1,))
        for step, _ in ONWARD[(0, 0)]:
            pass_c((0, 0), step, q)
    share(OWN, 0)
    share(OWN, 1)
    acc_r[...] = jnp.full(acc_r.shape, -1.0, jnp.float32)
    acc_c[...] = jnp.full(acc_c.shape, -1.0, jnp.float32)
    pl.semaphore_wait(corner_sem, 1)
    for q in (2, 3, 0, 1):
        pass_c((0, 0), (1, 1), q)

    step_z(1, 0)
    got_c((1, 0), 0)
    got_c((0, 1), 0)
    step_z(1, 1)
    got_c((1, 0), 1)
    got_c((0, 1), 1)
    got_c((3, 3), 2)
    step_z(1, 2)
    got_c((1, 0), 2)
    got_c((0, 1), 2)
    got_c((3, 3), 3)
    step_z(1, 3)
    got_c((1, 0), 3)
    got_c((0, 1), 3)
    got_c((3, 3), 0)
    ready_r(0, 1, -1)
    ready_c(OWN, 1)
    compute(6, 1, 0, 1)
    step_z(2, 0)
    got_c((2, 0), 0)
    got_c((0, 2), 0)
    got_c((3, 3), 1)
    ready_c(0, 2)
    compute(0, 2, 0, 1, -1)
    step_z(2, 1)
    got_c((2, 0), 1)
    got_c((0, 2), 1)
    got_c((2, 3), 2)
    got_c((1, 3), 0)
    step_z(2, 2)
    got_c((2, 3), 3)
    got_c((1, 3), 1)
    got_c((2, 0), 2)
    got_c((0, 2), 2)
    got_c((3, 2), 2)
    got_c((2, 3), 0)
    step_z(2, 3)
    got_c((2, 0), 3)
    got_c((0, 2), 3)
    ready_r(2, -2)
    compute(0, 2, 2, -2)
    got_c((3, 2), 3)
    got_c((2, 3), 1)
    step_z(3, 0)
    ready_c(7, 2)
    compute(7, 2, 0, 1, 2)
    got_c((3, 2), 0)
    got_c((1, 3), 2)
    step_z(3, 1)
    ready_c(2, 2)
    compute(2, 2, 0, 1, -1)
    got_c((3, 2), 1)
    got_c((1, 3), 3)
    step_z(3, 2)
    compute(2, 2, 2, -2)
    got_c((2, 2), 2, 0)
    step_z(3, 3)
    ready_c(4, 2)
    compute(4, 2, 0, 1, -1, 2, -2)
    got_c((2, 2), 3, 1)
    ready_r(3, -3)
    compute(0, 6, 3, -3)
    answer_r(-1, -2)
    compute(6, 3, 3)
    compute(6, 1, 2)
    got_z(4, 2)
    got_z(4, 0)
    ready_r(4)
    ready_c(9, 1)
    half[...] = product(wide(R, 7, 1, EARLY), wide(C, 0, 20, EARLY))
    compute(9, 1, 0, 1, 2, 3)
    answer_r(-3)
    got_z(4, 3)
    got_z(4, 1)
    use(half[...] + product(wide(R, 7, 1, LATE), wide(C, 0, 20, LATE)), 0, 10, (4,))
    answer_r(4)
    answer_c(9, 3, 5, 4, 7, 8, 2, 0, 1, 6)
    answer_r(3, 2, 1, 0)

    for d in sends:
        d.wait_send()
    best = jnp.maximum(out_r[0], acc_c[2 * OWN])
    for u in range(1, 8):
        arrived(res_r.at[u], rsem_r.at[u])
        best = jnp.maximum(best, res_r[u])
    for j in range(20):
        if j != 2 * OWN:
            arrived(res_c.at[j], rsem_c.at[j])
            best = jnp.maximum(best, res_c[j])
    out_ref[...] = jnp.max(best, axis=0, keepdims=True)


def shards(embeddings, cluster_ids, row_order):
    out = pl.pallas_call(
        kernel,
        out_shape=jax.ShapeDtypeStruct((1, 128), jnp.float32),
        in_specs=[pl.BlockSpec(memory_space=pltpu.HBM)] * 3,
        out_specs=pl.BlockSpec(memory_space=pltpu.VMEM),
        scratch_shapes=[
            pltpu.VMEM((128, 1024), jnp.bfloat16),
            pltpu.VMEM((1, 128), jnp.int32),
            pltpu.VMEM((1, 128), jnp.int32),
            pltpu.SemaphoreType.DMA((3,)),
            pltpu.VMEM((20, CHUNKS, 16, 128), jnp.bfloat16),
            pltpu.VMEM((8, CHUNKS, 16, 128), jnp.bfloat16),
            pltpu.VMEM((8, 128, 128), jnp.float32),
            pltpu.VMEM((20, 8, 128), jnp.float32),
            pltpu.VMEM((20, 8, 128), jnp.float32),
            pltpu.VMEM((128, 2560), jnp.float32),
            pltpu.VMEM((8, 128, 128), jnp.float32),
            pltpu.VMEM((20, 8, 128), jnp.float32),
            pltpu.VMEM((8, 8, 128), jnp.float32),
            pltpu.VMEM((8, 8, 128), jnp.float32),
            pltpu.VMEM((20, 8, 128), jnp.float32),
            pltpu.SemaphoreType.DMA((128,)),
            pltpu.SemaphoreType.DMA((10, 4)),
            pltpu.SemaphoreType.DMA((10, 2)),
            pltpu.SemaphoreType.DMA((8, 4)),
            pltpu.SemaphoreType.DMA((8,)),
            pltpu.SemaphoreType.DMA((20,)),
            pltpu.SemaphoreType.REGULAR,
        ],
        compiler_params=pltpu.CompilerParams(collective_id=0, has_side_effects=True, vmem_limit_bytes=64 << 20),
        name="nearest_earlier",
    )(embeddings, cluster_ids.reshape(1, 128), row_order.reshape(1, 128))
    return out.reshape(128)


def solution(mesh):
    in_specs = (P(("grp", "blk"), None), P(("grp", "blk")), P(("grp", "blk")))
    return jax.shard_map(shards, mesh=mesh, in_specs=in_specs, out_specs=P(("grp", "blk")), check_vma=False)
```

time: 206 us -> 44.2 us (0.21)
  blocking collectives: 107 us -> 0 us
  waiting for transfers between devices: 44 us -> 0 us
  Pallas kernels: 0 us -> 43 us
  matrix products: 16.4 us -> 0 us
  between operations: 13.5 us -> 0.02 us
  starting transfers between devices: 10.4 us -> 0 us
  other arithmetic: 6.65 us -> 0 us
  local copies, waits for them, and re-layouts: 7.43 us -> 1.1 us
    all_gather x2 -> x0, blocking collectives: 94.3 us -> none  [the longest x1 51.6 us: shards(): piece_order = lax.all_gather(local_order, 'blk', axis=0, tiled=True)]
    pallas_call x0 -> x1, Pallas kernels: none -> 43 us  [shards(): pl.pallas_call(kernel, out_shape=jax.ShapeDtypeStruct((1, 128), jnp.float...]
    all_gather x1 -> x0, waiting for transfers between devices: 34.9 us -> none  [shards(): piece_unit = lax.all_gather(local_unit, 'blk', axis=0, tiled=True)]
    dot_general x1 -> x0, matrix products: 16.4 us -> none  [pair_scores(): lax.dot_general(left, right, (((1,), (1,)), ((), ())), preferred_element_...]
    all_to_all x1 -> x0, blocking collectives: 12.7 us -> none  [shards(): lax.all_to_all(send_unit, 'grp', split_axis=0, concat_axis=0, tiled=True)]
    all_to_all x3 -> x0, starting transfers between devices: 10.4 us -> none  [the longest x1 3.97 us: shards(): lax.all_to_all(best.reshape(groups, capacity), 'grp', split_axis=0, conca...]
    all_to_all x3 -> x0, waiting for transfers between devices: 9.12 us -> none  [the longest x1 4.1 us: shards(): lax.all_to_all(best.reshape(groups, capacity), 'grp', split_axis=0, conca...]
    all_to_all x4 -> x0, local copies, waits for them, and re-layouts: 2.36 us -> none  [the longest x2 1.18 us: shards(): lax.all_to_all(send_order, 'grp', split_axis=0, concat_axis=0, tiled=True)]
  transfers between devices with their start and end apart: 4 -> 0, of which waited for: 4 -> 0; matrix products, arithmetic and copies ran while one was open for 2% -> 0% of each run, Pallas kernels for 0% -> 0%
where the time goes in v3:
time: 44.2 us; the launch traced here: 44.1 us
  Pallas kernels  43 us (97%)
  local copies, waits for them, and re-layouts  1.1 us (2%)
    pallas_call x1, Pallas kernels, shards(): pl.pallas_call(kernel, out_shape=jax.ShapeDtypeStruct((1, 128), jnp.float...  43 us
    unnamed x3, local copies, waits for them, and re-layouts  1.1 us

profile of v3, /device:TPU:1, one launch (start us, length us, event | category | flops | bytes accessed | tf_op | source)
XLA Modules:
  0.0 44.1 jit_solution(11225247073799541087)
XLA Ops:
  0.0 43.0 %nearest_earlier.1 = f32[1,128]{1,0:T(1,128)} custom-call(bf16[128,1024]{1,0:T(8,128)(2,1)} %emb_hbm.1, s32[1,128]{1,0:T(1,128)} %bitcast.3, s32[1,128]{1,0:T(1,128)} %bitcast.4), custom_call_target="tpu_custom_call" | custom-call | tf_op jit(solution)/shard_map/nearest_earlier/pallas_call | solution.py:298
  43.0 0.0 copy-start
  43.0 0.6 %copy-done = f32[1,128]{1,0:T(1,128)S(1)} copy-done((f32[1,128]{1,0:T(1,128)S(1)}, f32[1,128]{1,0:T(1,128)}, u32[]{:S(2)}) %copy-start) | copy-done | bytes 536
  43.6 0.5 %copy.5 = f32[128]{0:T(128)} copy(f32[128]{0:T(128)S(1)} %bitcast.5) | data formatting | bytes 1024
Async XLA Ops:
  43.0 0.6 %copy-start = (f32[1,128]{1,0:T(1,128)S(1)}, f32[1,128]{1,0:T(1,128)}, u32[]{:S(2)}) copy-start(f32[1,128]{1,0:T(1,128)} %nearest_earlier.1) | copy-start | bytes 1540

commit v4 on v3

--- a/solution.py
+++ b/solution.py
@@ -24,14 +24,16 @@
 }
 
 
-def wide(ref, start, count, features=range(8)):
-    return jnp.concatenate(
-        [ref[pl.ds(start, count), 1 + k * 8:9 + k * 8].reshape(count * 128, 128) for k in features], axis=1
-    )
-
-
-def product(left, right):
-    return lax.dot_general(left, right, (((1,), (1,)), ((), ())), preferred_element_type=jnp.float32)
+def rows_of(R, u, features=range(8)):
+    return jnp.concatenate([R[u, 1 + k * 8:9 + k * 8].reshape(128, 128) for k in features], axis=1)
+
+
+def columns_of(C, j, features=range(8)):
+    return jnp.concatenate([C[j, 1 + k * 8:9 + k * 8].reshape(128, 128) for k in features], axis=0)
+
+
+def product(rows, columns):
+    return jnp.dot(rows, columns, preferred_element_type=jnp.float32)
 
 
 def keys_of(tag):
@@ -68,11 +70,9 @@
         load.wait()
     values = emb_ref[...].astype(jnp.float32)
     total = jnp.sum(values * values, axis=1, keepdims=True)
-    unit = (values * lax.rsqrt(total + 1e-06)).astype(jnp.bfloat16)
+    unit = values * lax.rsqrt(total + 1e-06)
     for k in range(8):
-        piece = unit[:, k * 128:(k + 1) * 128].reshape(8, 16, 128)
-        C[2 * OWN, 1 + k * 8:9 + k * 8] = piece
-        R[0, 1 + k * 8:9 + k * 8] = piece
+        R[0, 1 + k * 8:9 + k * 8] = unit[:, k * 128:(k + 1) * 128].astype(jnp.bfloat16).reshape(8, 16, 128)
     row = lax.broadcasted_iota(jnp.int32, (16, 128), 0)
     order = ord_ref[...]
     tag = jnp.where(row == 0, cid_ref[...], jnp.where(row == 1, lax.shift_right_logical(order, 8), jnp.where(row == 2, order & 255, 0)))
@@ -138,8 +138,8 @@
         got_z(-k, (n + 2) % 4)
         got_z(k, n)
 
-    def ready_c(start, count):
-        for i in range(start, start + count):
+    def ready_c(*blocks):
+        for i in blocks:
             for h in range(2):
                 arrived(C.at[2 * i + 1, pl.ds(*HALVES[h])], ssem.at[i, h])
             for j in (2 * i, 2 * i + 1):
@@ -153,13 +153,13 @@
             _, high = keys_of(R[u, 0])
             row_key[u] = jnp.broadcast_to(high, (128, 128)).T
 
-    def use(scores, start, count, ks):
+    def use(scores, blocks, ks):
         for a, k in enumerate(ks):
             u = COLUMN.index(k)
             key = row_key[u]
             side = acc_r[u]
-            for b in range(2 * count):
-                j = 2 * start + b
+            for b in range(2 * len(blocks)):
+                j = 2 * blocks[b // 2] + b % 2
                 part = scores[a * 128:(a + 1) * 128, b * 128:(b + 1) * 128]
                 low = low_key[j, 0:1, :]
                 high = high_key[j, 0:1, :]
@@ -168,9 +168,13 @@
                 side = jnp.maximum(side, jnp.where((key > high) & (key < low + 32768.0), part, jnp.float32(-1.0)))
             acc_r[u] = side
 
-    def compute(start, count, *ks):
-        rows = jnp.concatenate([wide(R, COLUMN.index(k), 1) for k in ks], axis=0)
-        use(product(rows, wide(C, 2 * start, 2 * count)), start, count, ks)
+    def scores_of(blocks, ks, features=range(8)):
+        rows = jnp.concatenate([rows_of(R, COLUMN.index(k), features) for k in ks], axis=0)
+        columns = jnp.concatenate([columns_of(C, 2 * i + c, features) for i in blocks for c in range(2)], axis=1)
+        return product(rows, columns)
+
+    def compute(blocks, ks):
+        use(scores_of(blocks, ks), blocks, ks)
 
     def answer_r(*ks):
         for k in ks:
@@ -192,6 +196,9 @@
     for q in range(4):
         pass_z(0, (q + 2) % 4, (1,))
         pass_z(0, q, (-1,))
+    for k in range(8):
+        C[2 * OWN, 1 + k * 8:9 + k * 8] = unit[:, k * 128:(k + 1) * 128].T.astype(jnp.bfloat16).reshape(8, 16, 128)
+    for q in range(4):
         for step, _ in ONWARD[(0, 0)]:
             pass_c((0, 0), step, q)
     share(OWN, 0)
@@ -218,20 +225,21 @@
     got_c((0, 1), 3)
     got_c((3, 3), 0)
     ready_r(0, 1, -1)
-    ready_c(OWN, 1)
-    compute(6, 1, 0, 1)
+    ready_c(OWN)
     step_z(2, 0)
     got_c((2, 0), 0)
     got_c((0, 2), 0)
     got_c((3, 3), 1)
-    ready_c(0, 2)
-    compute(0, 2, 0, 1, -1)
+    ready_c(0, 1)
+    compute((6, 0, 1), (0, 1, -1))
     step_z(2, 1)
     got_c((2, 0), 1)
     got_c((0, 2), 1)
     got_c((2, 3), 2)
     got_c((1, 3), 0)
+    ready_c(2)
     step_z(2, 2)
+    compute((2,), (0, 1, -1))
     got_c((2, 3), 3)
     got_c((1, 3), 1)
     got_c((2, 0), 2)
@@ -242,43 +250,42 @@
     got_c((2, 0), 3)
     got_c((0, 2), 3)
     ready_r(2, -2)
-    compute(0, 2, 2, -2)
+    compute((6, 0, 1, 2), (2, -2))
     got_c((3, 2), 3)
     got_c((2, 3), 1)
     step_z(3, 0)
-    ready_c(7, 2)
-    compute(7, 2, 0, 1, 2)
+    ready_c(7, 8)
+    compute((7, 8), (0, 1, 2))
     got_c((3, 2), 0)
     got_c((1, 3), 2)
     step_z(3, 1)
-    ready_c(2, 2)
-    compute(2, 2, 0, 1, -1)
+    ready_c(3)
+    compute((3,), (0, 1, -1, 2, -2))
     got_c((3, 2), 1)
     got_c((1, 3), 3)
     step_z(3, 2)
-    compute(2, 2, 2, -2)
     got_c((2, 2), 2, 0)
+    ready_c(4, 5)
     step_z(3, 3)
-    ready_c(4, 2)
-    compute(4, 2, 0, 1, -1, 2, -2)
+    compute((4, 5), (0, 1, -1, 2, -2))
     got_c((2, 2), 3, 1)
     ready_r(3, -3)
-    compute(0, 6, 3, -3)
-    answer_r(-1, -2)
-    compute(6, 3, 3)
-    compute(6, 1, 2)
+    compute((0, 1, 2, 3, 4, 5), (3, -3))
+    answer_r(-1, -2, -3)
+    compute((6, 7, 8), (3,))
     got_z(4, 2)
     got_z(4, 0)
     ready_r(4)
-    ready_c(9, 1)
-    half[...] = product(wide(R, 7, 1, EARLY), wide(C, 0, 20, EARLY))
-    compute(9, 1, 0, 1, 2, 3)
-    answer_r(-3)
+    ready_c(9)
+    compute((9,), (0, 1, 2, 3))
+    every = tuple(range(10))
+    half[...] = scores_of(every, (4,), EARLY)
     got_z(4, 3)
     got_z(4, 1)
-    use(half[...] + product(wide(R, 7, 1, LATE), wide(C, 0, 20, LATE)), 0, 10, (4,))
+    use(half[...] + scores_of(every, (4,), LATE), every, (4,))
+    answer_c(9)
     answer_r(4)
-    answer_c(9, 3, 5, 4, 7, 8, 2, 0, 1, 6)
+    answer_c(3, 5, 4, 7, 8, 2, 0, 1, 6)
     answer_r(3, 2, 1, 0)
 
     for d in sends:

time: 44.2 us -> 42.6 us (0.964)
  Pallas kernels: 43 us -> 41.4 us
    pallas_call x1, Pallas kernels: 43 us -> 41.4 us  [shards(): pl.pallas_call(kernel, out_shape=jax.ShapeDtypeStruct((1, 128), jnp.float...]
where the time goes in v4:
time: 42.6 us; the launch traced here: 42.5 us
  Pallas kernels  41.4 us (97%)
  local copies, waits for them, and re-layouts  1.1 us (3%)
    pallas_call x1, Pallas kernels, shards(): pl.pallas_call(kernel, out_shape=jax.ShapeDtypeStruct((1, 128), jnp.float...  41.4 us
    unnamed x3, local copies, waits for them, and re-layouts  1.1 us

profile of v4, /device:TPU:1, one launch (start us, length us, event | category | flops | bytes accessed | tf_op | source)
XLA Modules:
  0.0 42.5 jit_solution(14627181925337175403)
XLA Ops:
  0.0 41.4 %nearest_earlier.1 = f32[1,128]{1,0:T(1,128)} custom-call(bf16[128,1024]{1,0:T(8,128)(2,1)} %emb_hbm.1, s32[1,128]{1,0:T(1,128)} %bitcast.3, s32[1,128]{1,0:T(1,128)} %bitcast.4), custom_call_target="tpu_custom_call" | custom-call | tf_op jit(solution)/shard_map/nearest_earlier/pallas_call | solution.py:305
  41.4 0.0 copy-start
  41.4 0.6 %copy-done = f32[1,128]{1,0:T(1,128)S(1)} copy-done((f32[1,128]{1,0:T(1,128)S(1)}, f32[1,128]{1,0:T(1,128)}, u32[]{:S(2)}) %copy-start) | copy-done | bytes 536
  42.0 0.5 %copy.5 = f32[128]{0:T(128)} copy(f32[128]{0:T(128)S(1)} %bitcast.5) | data formatting | bytes 1024
Async XLA Ops:
  41.4 0.6 %copy-start = (f32[1,128]{1,0:T(1,128)S(1)}, f32[1,128]{1,0:T(1,128)}, u32[]{:S(2)}) copy-start(f32[1,128]{1,0:T(1,128)} %nearest_earlier.1) | copy-start | bytes 1540

commit v5 on v4

--- a/solution.py
+++ b/solution.py
@@ -11,16 +11,16 @@
 HALVES = ((0, 33), (33, 32))
 QUARTERS = ((0, 17), (17, 16), (33, 16), (49, 16))
 EARLY, LATE = (0, 1, 4, 5), (2, 3, 6, 7)
-PLANE = ((1, 0), (0, 1), (3, 3), (2, 3), (1, 3), (3, 2), (0, 0), (2, 0), (0, 2), (2, 2))
+PLANE = ((1, 0), (0, 1), (3, 3), (2, 3), (1, 3), (1, 2), (0, 0), (0, 2), (2, 0), (2, 2))
 OWN = PLANE.index((0, 0))
 COLUMN = (0, 1, -1, 2, -2, 3, -3, 4)
 ONWARD = {
-    (0, 0): (((-1, 0), (0, 1, 2, 3)), ((0, -1), (0, 1, 2, 3))),
-    (1, 0): (((-1, 0), (0, 1, 2, 3)), ((0, 1), (0, 1))),
+    (0, 0): (((-1, 0), (0, 1, 2, 3)), ((0, -1), (2, 3, 0, 1))),
+    (1, 0): (((-1, 0), (0, 1)), ((0, 1), (0, 1))),
     (0, 1): (((0, -1), (0, 1, 2, 3)),),
-    (3, 3): (((1, 0), (0, 1, 2, 3)), ((0, 1), (0, 1, 2, 3))),
-    (2, 3): (((1, 0), (2, 3)), ((0, 1), (0, 1))),
-    (3, 2): (((1, 0), (2, 3)),),
+    (0, 2): (((-1, 0), (0, 1, 2, 3)),),
+    (3, 3): (((1, 0), (0, 1, 2, 3)),),
+    (2, 3): (((1, 0), (2, 3)), ((0, -1), (2, 3)), ((0, 1), (0, 1, 2, 3))),
 }
 
 
@@ -42,7 +42,7 @@
     return low, low + tag[1:2] * 256.0 + tag[2:3]
 
 
-def kernel(emb_hbm, cid_hbm, ord_hbm, out_ref, emb_ref, cid_ref, ord_ref, in_sems, C, R, row_key, low_key, high_key, half, acc_r, acc_c, out_r, res_r, res_c, send_sems, csem, ssem, zsem, rsem_r, rsem_c, corner_sem):
+def kernel(emb_hbm, cid_hbm, ord_hbm, out_ref, emb_ref, cid_ref, ord_ref, in_sems, C, R, row_low, row_key, low_key, high_key, half, acc_r, acc_c, out_r, res_r, res_c, send_sems, csem, ssem, zsem, rsem_r, rsem_c, corner_sem):
     loads = [
         pltpu.make_async_copy(src, dst, in_sems.at[i])
         for i, (src, dst) in enumerate(((emb_hbm, emb_ref), (cid_hbm, cid_ref), (ord_hbm, ord_ref)))
@@ -150,22 +150,27 @@
     def ready_r(*ks):
         for k in ks:
             u = COLUMN.index(k)
-            _, high = keys_of(R[u, 0])
+            low, high = keys_of(R[u, 0])
+            row_low[u] = jnp.broadcast_to(low, (128, 128)).T
             row_key[u] = jnp.broadcast_to(high, (128, 128)).T
+
+    def split(part, u, j):
+        same = jnp.where(row_low[u] == low_key[j, 0:1, :], part, jnp.float32(-1.0))
+        high = high_key[j, 0:1, :]
+        before = row_key[u] < high
+        if (u, j) == (0, 2 * OWN):
+            return jnp.where(row_key[u] > high, same, jnp.float32(-1.0)), jnp.where(before, same, jnp.float32(-1.0))
+        return jnp.where(before, jnp.float32(-1.0), same), jnp.where(before, same, jnp.float32(-1.0))
 
     def use(scores, blocks, ks):
         for a, k in enumerate(ks):
             u = COLUMN.index(k)
-            key = row_key[u]
             side = acc_r[u]
             for b in range(2 * len(blocks)):
                 j = 2 * blocks[b // 2] + b % 2
-                part = scores[a * 128:(a + 1) * 128, b * 128:(b + 1) * 128]
-                low = low_key[j, 0:1, :]
-                high = high_key[j, 0:1, :]
-                earlier = jnp.where((key >= low) & (key < high), part, jnp.float32(-1.0))
+                later, earlier = split(scores[a * 128:(a + 1) * 128, b * 128:(b + 1) * 128], u, j)
                 acc_c[j] = jnp.maximum(acc_c[j], jnp.max(earlier.reshape(16, 8, 128), axis=0))
-                side = jnp.maximum(side, jnp.where((key > high) & (key < low + 32768.0), part, jnp.float32(-1.0)))
+                side = jnp.maximum(side, later)
             acc_r[u] = side
 
     def scores_of(blocks, ks, features=range(8)):
@@ -199,8 +204,8 @@
     for k in range(8):
         C[2 * OWN, 1 + k * 8:9 + k * 8] = unit[:, k * 128:(k + 1) * 128].T.astype(jnp.bfloat16).reshape(8, 16, 128)
     for q in range(4):
-        for step, _ in ONWARD[(0, 0)]:
-            pass_c((0, 0), step, q)
+        for step, order in ONWARD[(0, 0)]:
+            pass_c((0, 0), step, order[q])
     share(OWN, 0)
     share(OWN, 1)
     acc_r[...] = jnp.full(acc_r.shape, -1.0, jnp.float32)
@@ -211,81 +216,86 @@
 
     step_z(1, 0)
     got_c((1, 0), 0)
-    got_c((0, 1), 0)
+    got_c((0, 1), 2)
     step_z(1, 1)
     got_c((1, 0), 1)
-    got_c((0, 1), 1)
+    got_c((0, 1), 3)
     got_c((3, 3), 2)
     step_z(1, 2)
+    got_c((0, 1), 0)
     got_c((1, 0), 2)
-    got_c((0, 1), 2)
     got_c((3, 3), 3)
     step_z(1, 3)
+    got_c((0, 1), 1)
     got_c((1, 0), 3)
-    got_c((0, 1), 3)
     got_c((3, 3), 0)
     ready_r(0, 1, -1)
     ready_c(OWN)
     step_z(2, 0)
-    got_c((2, 0), 0)
-    got_c((0, 2), 0)
+    got_c((0, 2), 2)
     got_c((3, 3), 1)
     ready_c(0, 1)
     compute((6, 0, 1), (0, 1, -1))
     step_z(2, 1)
-    got_c((2, 0), 1)
-    got_c((0, 2), 1)
     got_c((2, 3), 2)
-    got_c((1, 3), 0)
+    got_c((0, 2), 3)
     ready_c(2)
     step_z(2, 2)
     compute((2,), (0, 1, -1))
     got_c((2, 3), 3)
-    got_c((1, 3), 1)
-    got_c((2, 0), 2)
-    got_c((0, 2), 2)
-    got_c((3, 2), 2)
+    got_c((0, 2), 0)
     got_c((2, 3), 0)
     step_z(2, 3)
-    got_c((2, 0), 3)
-    got_c((0, 2), 3)
+    got_c((0, 2), 1)
     ready_r(2, -2)
     compute((6, 0, 1, 2), (2, -2))
-    got_c((3, 2), 3)
     got_c((2, 3), 1)
+    got_c((1, 3), 0, 1)
     step_z(3, 0)
-    ready_c(7, 8)
-    compute((7, 8), (0, 1, 2))
-    got_c((3, 2), 0)
-    got_c((1, 3), 2)
+    ready_c(7)
+    compute((7,), (0, 1, 2))
+    got_c((2, 0), 0, 1, 2)
+    got_c((1, 2), 2)
     step_z(3, 1)
     ready_c(3)
     compute((3,), (0, 1, -1, 2, -2))
-    got_c((3, 2), 1)
+    got_c((2, 0), 3)
+    got_c((1, 2), 3)
+    got_c((1, 3), 2)
+    step_z(3, 2)
+    ready_c(8)
+    compute((8,), (0, 1, 2))
     got_c((1, 3), 3)
-    step_z(3, 2)
-    got_c((2, 2), 2, 0)
+    got_c((1, 2), 0, 1)
+    step_z(3, 3)
+    got_c((2, 2), 2, 3)
+    ready_r(3, -3)
+    compute((0, 1, 2, 3), (3, -3))
+    got_c((2, 2), 0, 1)
     ready_c(4, 5)
-    step_z(3, 3)
-    compute((4, 5), (0, 1, -1, 2, -2))
-    got_c((2, 2), 3, 1)
-    ready_r(3, -3)
-    compute((0, 1, 2, 3, 4, 5), (3, -3))
+    compute((4, 5), (0, 1, -1, 2, -2, 3, -3))
     answer_r(-1, -2, -3)
-    compute((6, 7, 8), (3,))
+    ready_c(9)
+    compute((6, 7, 8, 9), (3,))
+    compute((9,), (0, 1, 2))
     got_z(4, 2)
     got_z(4, 0)
     ready_r(4)
-    ready_c(9)
-    compute((9,), (0, 1, 2, 3))
     every = tuple(range(10))
     half[...] = scores_of(every, (4,), EARLY)
     got_z(4, 3)
     got_z(4, 1)
-    use(half[...] + scores_of(every, (4,), LATE), every, (4,))
-    answer_c(9)
+    half[...] += scores_of(every, (4,), LATE)
+    side = acc_r[7]
+    for j in range(20):
+        side = jnp.maximum(side, split(half[:, j * 128:(j + 1) * 128], 7, j)[0])
+    acc_r[7] = side
     answer_r(4)
-    answer_c(3, 5, 4, 7, 8, 2, 0, 1, 6)
+    for i in (9, 3, 5, 4, 7, 8, 2, 0, 1, 6):
+        for j in (2 * i, 2 * i + 1):
+            earlier = split(half[:, j * 128:(j + 1) * 128], 7, j)[1]
+            acc_c[j] = jnp.maximum(acc_c[j], jnp.max(earlier.reshape(16, 8, 128), axis=0))
+        answer_c(i)
     answer_r(3, 2, 1, 0)
 
     for d in sends:
@@ -314,6 +324,7 @@
             pltpu.SemaphoreType.DMA((3,)),
             pltpu.VMEM((20, CHUNKS, 16, 128), jnp.bfloat16),
             pltpu.VMEM((8, CHUNKS, 16, 128), jnp.bfloat16),
+            pltpu.VMEM((8, 128, 128), jnp.float32),
             pltpu.VMEM((8, 128, 128), jnp.float32),
             pltpu.VMEM((20, 8, 128), jnp.float32),
             pltpu.VMEM((20, 8, 128), jnp.float32),

time: 42.6 us -> 42.1 us (0.988)
  Pallas kernels: 41.4 us -> 40.9 us
    pallas_call x1, Pallas kernels: 41.4 us -> 40.9 us  [shards(): pl.pallas_call(kernel, out_shape=jax.ShapeDtypeStruct((1, 128), jnp.float...]
where the time goes in v5:
time: 42.1 us; the launch traced here: 42 us
  Pallas kernels  40.9 us (97%)
  local copies, waits for them, and re-layouts  1.1 us (3%)
    pallas_call x1, Pallas kernels, shards(): pl.pallas_call(kernel, out_shape=jax.ShapeDtypeStruct((1, 128), jnp.float...  40.9 us
    unnamed x3, local copies, waits for them, and re-layouts  1.1 us

profile of v5, /device:TPU:1, one launch (start us, length us, event | category | flops | bytes accessed | tf_op | source)
XLA Modules:
  0.0 42.0 jit_solution(3237767827605352928)
XLA Ops:
  0.0 40.9 %nearest_earlier.1 = f32[1,128]{1,0:T(1,128)} custom-call(bf16[128,1024]{1,0:T(8,128)(2,1)} %emb_hbm.1, s32[1,128]{1,0:T(1,128)} %bitcast.3, s32[1,128]{1,0:T(1,128)} %bitcast.4), custom_call_target="tpu_custom_call" | custom-call | tf_op jit(solution)/shard_map/nearest_earlier/pallas_call | solution.py:315
  40.9 0.0 copy-start
  40.9 0.6 %copy-done = f32[1,128]{1,0:T(1,128)S(1)} copy-done((f32[1,128]{1,0:T(1,128)S(1)}, f32[1,128]{1,0:T(1,128)}, u32[]{:S(2)}) %copy-start) | copy-done | bytes 536
  41.5 0.5 %copy.5 = f32[128]{0:T(128)} copy(f32[128]{0:T(128)S(1)} %bitcast.5) | data formatting | bytes 1024
Async XLA Ops:
  40.9 0.6 %copy-start = (f32[1,128]{1,0:T(1,128)S(1)}, f32[1,128]{1,0:T(1,128)}, u32[]{:S(2)}) copy-start(f32[1,128]{1,0:T(1,128)} %nearest_earlier.1) | copy-start | bytes 1540

commit v6 on v5

--- a/solution.py
+++ b/solution.py
@@ -42,13 +42,9 @@
     return low, low + tag[1:2] * 256.0 + tag[2:3]
 
 
-def kernel(emb_hbm, cid_hbm, ord_hbm, out_ref, emb_ref, cid_ref, ord_ref, in_sems, C, R, row_low, row_key, low_key, high_key, half, acc_r, acc_c, out_r, res_r, res_c, send_sems, csem, ssem, zsem, rsem_r, rsem_c, corner_sem):
-    loads = [
-        pltpu.make_async_copy(src, dst, in_sems.at[i])
-        for i, (src, dst) in enumerate(((emb_hbm, emb_ref), (cid_hbm, cid_ref), (ord_hbm, ord_ref)))
-    ]
-    for load in loads:
-        load.start()
+def kernel(emb_hbm, cid_ref, ord_ref, out_ref, emb_ref, in_sem, C, R, row_low, row_key, low_key, high_key, half, acc_r, acc_c, out_r, res_r, res_c, send_sems, csem, ssem, zsem, rsem_r, rsem_c, corner_sem):
+    load = pltpu.make_async_copy(emb_hbm, emb_ref, in_sem)
+    load.start()
     x = lax.axis_index("grp")
     blk = lax.axis_index("blk")
     core = lax.rem(blk, 2)
@@ -66,8 +62,7 @@
     for target in near:
         pl.semaphore_signal(barrier, inc=1, device_id=target, device_id_type=MESH)
 
-    for load in loads:
-        load.wait()
+    load.wait()
     values = emb_ref[...].astype(jnp.float32)
     total = jnp.sum(values * values, axis=1, keepdims=True)
     unit = values * lax.rsqrt(total + 1e-06)
@@ -275,12 +270,12 @@
     ready_c(4, 5)
     compute((4, 5), (0, 1, -1, 2, -2, 3, -3))
     answer_r(-1, -2, -3)
-    ready_c(9)
-    compute((6, 7, 8, 9), (3,))
-    compute((9,), (0, 1, 2))
+    compute((6, 7, 8), (3,))
     got_z(4, 2)
     got_z(4, 0)
     ready_r(4)
+    ready_c(9)
+    compute((9,), (0, 1, 2, 3))
     every = tuple(range(10))
     half[...] = scores_of(every, (4,), EARLY)
     got_z(4, 3)
@@ -290,13 +285,13 @@
     for j in range(20):
         side = jnp.maximum(side, split(half[:, j * 128:(j + 1) * 128], 7, j)[0])
     acc_r[7] = side
-    answer_r(4)
+    answer_r(4, 3)
     for i in (9, 3, 5, 4, 7, 8, 2, 0, 1, 6):
         for j in (2 * i, 2 * i + 1):
             earlier = split(half[:, j * 128:(j + 1) * 128], 7, j)[1]
             acc_c[j] = jnp.maximum(acc_c[j], jnp.max(earlier.reshape(16, 8, 128), axis=0))
         answer_c(i)
-    answer_r(3, 2, 1, 0)
+    answer_r(2, 1, 0)
 
     for d in sends:
         d.wait_send()
@@ -315,13 +310,11 @@
     out = pl.pallas_call(
         kernel,
         out_shape=jax.ShapeDtypeStruct((1, 128), jnp.float32),
-        in_specs=[pl.BlockSpec(memory_space=pltpu.HBM)] * 3,
+        in_specs=[pl.BlockSpec(memory_space=pltpu.HBM)] + [pl.BlockSpec(memory_space=pltpu.VMEM)] * 2,
         out_specs=pl.BlockSpec(memory_space=pltpu.VMEM),
         scratch_shapes=[
             pltpu.VMEM((128, 1024), jnp.bfloat16),
-            pltpu.VMEM((1, 128), jnp.int32),
-            pltpu.VMEM((1, 128), jnp.int32),
-            pltpu.SemaphoreType.DMA((3,)),
+            pltpu.SemaphoreType.DMA,
             pltpu.VMEM((20, CHUNKS, 16, 128), jnp.bfloat16),
             pltpu.VMEM((8, CHUNKS, 16, 128), jnp.bfloat16),
             pltpu.VMEM((8, 128, 128), jnp.float32),
@@ -342,7 +335,7 @@
             pltpu.SemaphoreType.DMA((20,)),
             pltpu.SemaphoreType.REGULAR,
         ],
-        compiler_params=pltpu.CompilerParams(collective_id=0, has_side_effects=True, vmem_limit_bytes=64 << 20),
+        compiler_params=pltpu.CompilerParams(collective_id=0, has_side_effects=True, vmem_limit_bytes=56475648),
         name="nearest_earlier",
     )(embeddings, cluster_ids.reshape(1, 128), row_order.reshape(1, 128))
     return out.reshape(128)

time: 42.1 us -> 41.7 us (level)
  Pallas kernels: 40.9 us -> 40.4 us
    pallas_call x1, Pallas kernels: 40.9 us -> 40.4 us  [shards(): pl.pallas_call(kernel, out_shape=jax.ShapeDtypeStruct((1, 128), jnp.float...]
    unnamed x3 -> x5, local copies, waits for them, and re-layouts: 1.1 us -> 1.18 us
where the time goes in v6:
time: 41.7 us; the launch traced here: 41.6 us
  Pallas kernels  40.4 us (97%)
  local copies, waits for them, and re-layouts  1.18 us (3%)
    pallas_call x1, Pallas kernels, shards(): pl.pallas_call(kernel, out_shape=jax.ShapeDtypeStruct((1, 128), jnp.float...  40.4 us
    unnamed x5, local copies, waits for them, and re-layouts  1.18 us

profile of v6, /device:TPU:1, one launch (start us, length us, event | category | flops | bytes accessed | tf_op | source)
XLA Modules:
  0.0 41.6 jit_solution(2067163182911007604)
XLA Ops:
  0.0 0.0 copy-start
  0.0 0.0 copy-start.1
  0.0 0.7 %copy-done = s32[128]{0:T(128)S(1)} copy-done((s32[128]{0:T(128)S(1)}, s32[128]{0:T(128)}, u32[]{:S(2)}) %copy-start) | copy-done | bytes 536
  0.7 0.0 copy-done.1
  0.7 40.4 %nearest_earlier.1 = f32[1,128]{1,0:T(1,128)S(1)} custom-call(bf16[128,1024]{1,0:T(8,128)(2,1)} %emb_hbm.1, s32[1,128]{1,0:T(1,128)S(1)} %bitcast.3, s32[1,128]{1,0:T(1,128)S(1)} %bitcast.4), custom_call_target="tpu_custom_call" | custom-call | tf_op jit(solution)/shard_map/nearest_earlier/pallas_call | solution.py:310
  41.1 0.5 %copy.5 = f32[128]{0:T(128)} copy(f32[128]{0:T(128)S(1)} %bitcast.5) | data formatting | bytes 1024
Async XLA Ops:
  0.0 0.7 %copy-start = (s32[128]{0:T(128)S(1)}, s32[128]{0:T(128)}, u32[]{:S(2)}) copy-start(s32[128]{0:T(128)} %param.4) | copy-start | bytes 1540
  0.0 0.7 %copy-start.1 = (s32[128]{0:T(128)S(1)}, s32[128]{0:T(128)}, u32[]{:S(2)}) copy-start(s32[128]{0:T(128)} %param.5) | copy-start | bytes 1540

commit v7 on v6

--- a/solution.py
+++ b/solution.py
@@ -269,7 +269,6 @@
     got_c((2, 2), 0, 1)
     ready_c(4, 5)
     compute((4, 5), (0, 1, -1, 2, -2, 3, -3))
-    answer_r(-1, -2, -3)
     compute((6, 7, 8), (3,))
     got_z(4, 2)
     got_z(4, 0)
@@ -285,13 +284,15 @@
     for j in range(20):
         side = jnp.maximum(side, split(half[:, j * 128:(j + 1) * 128], 7, j)[0])
     acc_r[7] = side
-    answer_r(4, 3)
+    answer_r(4)
     for i in (9, 3, 5, 4, 7, 8, 2, 0, 1, 6):
         for j in (2 * i, 2 * i + 1):
             earlier = split(half[:, j * 128:(j + 1) * 128], 7, j)[1]
             acc_c[j] = jnp.maximum(acc_c[j], jnp.max(earlier.reshape(16, 8, 128), axis=0))
         answer_c(i)
-    answer_r(2, 1, 0)
+        if i == 9:
+            answer_r(3, -3)
+    answer_r(2, -2, 1, -1, 0)
 
     for d in sends:
         d.wait_send()

time: 41.7 us -> 41.4 us (level)
  no operation moved by 1% of the time
where the time goes in v7:
time: 41.4 us; the launch traced here: 41.3 us
  Pallas kernels  40.1 us (97%)
  local copies, waits for them, and re-layouts  1.18 us (3%)
    pallas_call x1, Pallas kernels, shards(): pl.pallas_call(kernel, out_shape=jax.ShapeDtypeStruct((1, 128), jnp.float...  40.1 us
    unnamed x5, local copies, waits for them, and re-layouts  1.18 us

profile of v7, /device:TPU:1, one launch (start us, length us, event | category | flops | bytes accessed | tf_op | source)
XLA Modules:
  0.0 41.3 jit_solution(1974401509528050715)
XLA Ops:
  0.0 0.0 copy-start
  0.0 0.0 copy-start.1
  0.0 0.7 %copy-done = s32[128]{0:T(128)S(1)} copy-done((s32[128]{0:T(128)S(1)}, s32[128]{0:T(128)}, u32[]{:S(2)}) %copy-start) | copy-done | bytes 536
  0.7 0.0 copy-done.1
  0.7 40.1 %nearest_earlier.1 = f32[1,128]{1,0:T(1,128)S(1)} custom-call(bf16[128,1024]{1,0:T(8,128)(2,1)} %emb_hbm.1, s32[1,128]{1,0:T(1,128)S(1)} %bitcast.3, s32[1,128]{1,0:T(1,128)S(1)} %bitcast.4), custom_call_target="tpu_custom_call" | custom-call | tf_op jit(solution)/shard_map/nearest_earlier/pallas_call | solution.py:311
  40.7 0.5 %copy.5 = f32[128]{0:T(128)} copy(f32[128]{0:T(128)S(1)} %bitcast.5) | data formatting | bytes 1024
Async XLA Ops:
  0.0 0.7 %copy-start = (s32[128]{0:T(128)S(1)}, s32[128]{0:T(128)}, u32[]{:S(2)}) copy-start(s32[128]{0:T(128)} %param.4) | copy-start | bytes 1540
  0.0 0.7 %copy-start.1 = (s32[128]{0:T(128)S(1)}, s32[128]{0:T(128)}, u32[]{:S(2)}) copy-start(s32[128]{0:T(128)} %param.5) | copy-start | bytes 1540

commit v8 on v7

--- a/solution.py
+++ b/solution.py
@@ -290,7 +290,7 @@
             earlier = split(half[:, j * 128:(j + 1) * 128], 7, j)[1]
             acc_c[j] = jnp.maximum(acc_c[j], jnp.max(earlier.reshape(16, 8, 128), axis=0))
         answer_c(i)
-        if i == 9:
+        if i == 5:
             answer_r(3, -3)
     answer_r(2, -2, 1, -1, 0)
 

time: 41.4 us -> 41.4 us (level)
  no operation moved by 1% of the time
where the time goes in v8:
time: 41.4 us; the launch traced here: 41.3 us
  Pallas kernels  40.1 us (97%)
  local copies, waits for them, and re-layouts  1.18 us (3%)
    pallas_call x1, Pallas kernels, shards(): pl.pallas_call(kernel, out_shape=jax.ShapeDtypeStruct((1, 128), jnp.float...  40.1 us
    unnamed x5, local copies, waits for them, and re-layouts  1.18 us

profile of v8, /device:TPU:1, one launch (start us, length us, event | category | flops | bytes accessed | tf_op | source)
XLA Modules:
  0.0 41.3 jit_solution(17465422902774940067)
XLA Ops:
  0.0 0.0 copy-start
  0.0 0.0 copy-start.1
  0.0 0.7 %copy-done = s32[128]{0:T(128)S(1)} copy-done((s32[128]{0:T(128)S(1)}, s32[128]{0:T(128)}, u32[]{:S(2)}) %copy-start) | copy-done | bytes 536
  0.7 0.0 copy-done.1
  0.7 40.1 %nearest_earlier.1 = f32[1,128]{1,0:T(1,128)S(1)} custom-call(bf16[128,1024]{1,0:T(8,128)(2,1)} %emb_hbm.1, s32[1,128]{1,0:T(1,128)S(1)} %bitcast.3, s32[1,128]{1,0:T(1,128)S(1)} %bitcast.4), custom_call_target="tpu_custom_call" | custom-call | tf_op jit(solution)/shard_map/nearest_earlier/pallas_call | solution.py:311
  40.7 0.5 %copy.5 = f32[128]{0:T(128)} copy(f32[128]{0:T(128)S(1)} %bitcast.5) | data formatting | bytes 1024
Async XLA Ops:
  0.0 0.7 %copy-start = (s32[128]{0:T(128)S(1)}, s32[128]{0:T(128)}, u32[]{:S(2)}) copy-start(s32[128]{0:T(128)} %param.4) | copy-start | bytes 1540
  0.0 0.7 %copy-start.1 = (s32[128]{0:T(128)S(1)}, s32[128]{0:T(128)}, u32[]{:S(2)}) copy-start(s32[128]{0:T(128)} %param.5) | copy-start | bytes 1540
